TPU v7x, 32 devices: a whole 2x2x4 slice. The times are simulated.
32 devices in a mesh: fsdp: 8 (over z, y), ctx: 2 (over x), tp: 2 (over core).
Axes of the slice: x: 2, y: 2, z: 4, core: 2. Of those that a mesh axis runs over, the one named last changes fastest.
Arguments:
- inputs: bfloat16 [32, 580, 1024], P('fsdp', 'ctx'), may hold values from -6 to 6
- cotangent: bfloat16 [32, 580, 1024], P('fsdp', 'ctx'), may hold values from -9 to 9
- key_mask: int32 [32, 580], P('fsdp', 'ctx'), may hold values from 0 to 1, as said below
- image_mask: int32 [32], P('fsdp'), may hold values 0 or 1
- qkv_weight: float32 [1024, 3, 1024], P('fsdp', None, 'tp'), may hold values from -0.1875 to 0.1875
- out_weight: float32 [1024, 1024], P('tp', 'fsdp'), may hold values from -2.5 to 2.5
- up_weight: float32 [1024, 4096], P('fsdp', 'tp'), may hold values from -0.1875 to 0.1875
- down_weight: float32 [4096, 1024], P('tp', 'fsdp'), may hold values from -1 to 1
- vectors: float32 [12, 1024], replicated, may hold values from -2 to 2
- row_qkv: float32 [1024], P('fsdp'), may hold values from 4640 to 18560
- col_qkv: float32 [3, 1024], P(None, 'tp'), may hold values from 4640 to 18560
- row_out: float32 [1024], P('tp'), may hold values from 257 to 1030
- col_out: float32 [1024], P('fsdp'), may hold values from 257 to 1030
- row_up: float32 [1024], P('fsdp'), may hold values from 3093 to 12373
- col_up: float32 [4096], P('tp'), may hold values from 3093 to 12373
- row_down: float32 [4096], P('tp'), may hold values from 12992 to 55680
- col_down: float32 [1024], P('fsdp'), may hold values from 12992 to 55680
- vector_moments: float32 [12, 1024], replicated, may hold values from 3712 to 37120
Outputs:
- output: bfloat16 [32, 580, 1024], P('fsdp', 'ctx')
- input_grad: bfloat16 [32, 580, 1024], P('fsdp', 'ctx')
- qkv_grad: float32 [1024, 3, 1024], P('fsdp', None, 'tp')
- out_grad: float32 [1024, 1024], P('tp', 'fsdp')
- up_grad: float32 [1024, 4096], P('fsdp', 'tp')
- down_grad: float32 [4096, 1024], P('tp', 'fsdp')
- vector_grad: float32 [12, 1024], replicated
- qkv_new: float32 [1024, 3, 1024], P('fsdp', None, 'tp')
- out_new: float32 [1024, 1024], P('tp', 'fsdp')
- up_new: float32 [1024, 4096], P('fsdp', 'tp')
- down_new: float32 [4096, 1024], P('tp', 'fsdp')
- vector_new: float32 [12, 1024], replicated
- qkv_copy: bfloat16 [1024, 3, 1024], P('fsdp', None, 'tp')
- out_copy: bfloat16 [1024, 1024], P('tp', 'fsdp')
- up_copy: bfloat16 [1024, 4096], P('fsdp', 'tp')
- down_copy: bfloat16 [4096, 1024], P('tp', 'fsdp')
- qkv_rows: float32 [1024], P('fsdp')
- qkv_cols: float32 [3, 1024], P(None, 'tp')
- out_rows: float32 [1024], P('tp')
- out_cols: float32 [1024], P('fsdp')
- up_rows: float32 [1024], P('fsdp')
- up_cols: float32 [4096], P('tp')
- down_rows: float32 [4096], P('tp')
- down_cols: float32 [1024], P('fsdp')
- vector_moment: float32 [12, 1024], replicated
Inputs may be any that keep to these rules, and one draw needn't show every extreme that they name: `key_mask`: each image's real slots are its first ones, at least 577 of them.
All inputs are finite; a program needn't handle non-finite values. No bound on the sum of `image_mask` on one device may be relied on, other than what follows from the above.
Results may differ from a plain program's by a relative error of at most 0.017.
Values may be sent and summed in bfloat16 or wider, within the bound.
A program may use at most 256 MiB of HBM per device.

v0:
```python
import jax
import jax.numpy as jnp
from jax import lax
from jax.sharding import PartitionSpec as P

HD = 64
FF = 4096


eps_norm = 1e-06
decay_rate = 0.5
clip_level = 0.1
step_rate = 5.0


def norm_rows(rows, scale_row, offset):
    row_mean = jnp.mean(rows, -1, keepdims=True)
    centered = rows - row_mean
    inverse = lax.rsqrt(jnp.mean(centered * centered, -1, keepdims=True) + eps_norm)
    normal = centered * inverse
    return (normal * scale_row + offset, normal, inverse)


def norm_back(grad_rows, normal, inverse, scale_row):
    scaled = grad_rows * scale_row
    first_term = jnp.mean(scaled, -1, keepdims=True)
    second_term = jnp.mean(scaled * normal, -1, keepdims=True)
    return inverse * (scaled - first_term - normal * second_term)


def gelu_erf(argument):
    return 0.5 * argument * (1.0 + lax.erf(argument * 0.7071067811865476))


def gelu_slope(argument):
    return (
        0.5 * (1.0 + lax.erf(argument * 0.7071067811865476))
        + argument * jnp.exp(-0.5 * argument * argument) * 0.3989422804014327
    )


def masked_scores(queries, key_rows, valid_keys):
    scale_qk = queries.shape[-1] ** (-0.5)
    scores = (
        jnp.einsum("gqhe,gkhe->ghqk", queries, key_rows, preferred_element_type=jnp.float32)
        * scale_qk
    )
    return jnp.where(valid_keys[:, None, None, :] > 0, scores, -1000000000.0)


def attend_forward(pieces):
    queries, key_rows, value_rows, valid_keys = pieces
    scores = masked_scores(queries, key_rows, valid_keys)
    row_max = jnp.max(scores, -1, keepdims=True)
    exponent = jnp.exp(scores - row_max)
    totals = jnp.sum(exponent, -1, keepdims=True)
    attention = (exponent / totals).astype(jnp.bfloat16)
    attended = jnp.einsum(
        "ghqk,gkhe->gqhe", attention, value_rows, preferred_element_type=jnp.float32
    )
    return (attended.astype(jnp.bfloat16), (row_max + jnp.log(totals))[..., 0])


def attend_back(pieces):
    queries, key_rows, value_rows, valid_keys, logsum, grad_heads = pieces
    scale_qk = queries.shape[-1] ** (-0.5)
    scores = masked_scores(queries, key_rows, valid_keys)
    attention = jnp.exp(scores - logsum[..., None])
    grad_attention = jnp.einsum(
        "gqhe,gkhe->ghqk", grad_heads, value_rows, preferred_element_type=jnp.float32
    )
    inner = jnp.sum(attention * grad_attention, -1, keepdims=True)
    grad_scores = (attention * (grad_attention - inner)).astype(jnp.bfloat16)
    grad_queries = (
        jnp.einsum("ghqk,gkhe->gqhe", grad_scores, key_rows, preferred_element_type=jnp.float32)
        * scale_qk
    ).astype(jnp.bfloat16)
    grad_keys = (
        jnp.einsum("ghqk,gqhe->gkhe", grad_scores, queries, preferred_element_type=jnp.float32)
        * scale_qk
    )
    grad_values = jnp.einsum(
        "ghqk,gqhe->gkhe",
        attention.astype(jnp.bfloat16),
        grad_heads,
        preferred_element_type=jnp.float32,
    )
    return (grad_queries, grad_keys, grad_values)


def place_at(piece, full_shape, start, axis):
    return lax.dynamic_update_slice_in_dim(jnp.zeros(full_shape, jnp.float32), piece, start, axis)


def factor_local(
    grad_local, rows_old, cols_old, rows_full, rows_here, cols_here, row_total, col_total, old_total
):
    rows_new = decay_rate * rows_old + (1.0 - decay_rate) * rows_here / col_total
    cols_new = decay_rate * cols_old + (1.0 - decay_rate) * cols_here / row_total
    rows_avg = decay_rate * old_total / row_total + (1.0 - decay_rate) * jnp.sum(rows_full) / (
        row_total * col_total
    )
    update = grad_local * lax.rsqrt(rows_new[:, None] * cols_new[None, :] / rows_avg)
    return (rows_new, cols_new, update)


def body(
    inputs,
    cotangent,
    key_mask,
    image_mask,
    qkv_weight,
    out_weight,
    up_weight,
    down_weight,
    vectors,
    row_qkv,
    col_qkv,
    row_out,
    col_out,
    row_up,
    col_up,
    row_down,
    col_down,
    vector_moments,
):
    images, local_tokens, model_width = inputs.shape
    rows_here = images * local_tokens
    width_piece = qkv_weight.shape[0]
    half_width = qkv_weight.shape[2]
    half_hidden = up_weight.shape[1]
    head_size = HD
    heads_here = half_width // head_size
    tp_index = lax.axis_index("tp")
    fsdp_index = lax.axis_index("fsdp")
    tp_first = (tp_index == 0).astype(jnp.float32)
    ctx_first = (lax.axis_index("ctx") == 0).astype(jnp.float32)
    fsdp_first = (fsdp_index == 0).astype(jnp.float32)
    mix_w, out_w, up_w, down_w = (
        lax.all_gather(qkv_weight.astype(jnp.bfloat16), "fsdp", axis=0, tiled=True),
        lax.all_gather(out_weight.astype(jnp.bfloat16), "fsdp", axis=1, tiled=True),
        lax.all_gather(up_weight.astype(jnp.bfloat16), "fsdp", axis=0, tiled=True),
        lax.all_gather(down_weight.astype(jnp.bfloat16), "fsdp", axis=1, tiled=True),
    )
    query_bias = lax.dynamic_slice_in_dim(vectors[2], tp_index * half_width, half_width)
    value_bias = lax.dynamic_slice_in_dim(vectors[3], tp_index * half_width, half_width)
    up_bias = lax.dynamic_slice_in_dim(vectors[8:].reshape(-1), tp_index * half_hidden, half_hidden)
    flat_rows = inputs.astype(jnp.float32).reshape(rows_here, model_width)
    normed, normal_one, inverse_one = norm_rows(flat_rows, vectors[0], vectors[1])
    normed_low = normed.astype(jnp.bfloat16)
    projected = jnp.einsum("td,dcn->tcn", normed_low, mix_w, preferred_element_type=jnp.float32)
    queries = (projected[:, 0] + query_bias).astype(jnp.bfloat16)
    key_low = projected[:, 1].astype(jnp.bfloat16).reshape(images, local_tokens, half_width)
    value_low = (
        (projected[:, 2] + value_bias)
        .astype(jnp.bfloat16)
        .reshape(images, local_tokens, half_width)
    )
    all_keys, all_values, all_valid = (
        lax.all_gather(key_low, "ctx", axis=1, tiled=True),
        lax.all_gather(value_low, "ctx", axis=1, tiled=True),
        lax.all_gather(key_mask.astype(jnp.bfloat16), "ctx", axis=1, tiled=True),
    )
    seq_all = all_keys.shape[1]
    group_size = min(2, images)
    groups = images // group_size

    def grouped(array):
        return array.reshape((groups, group_size) + array.shape[1:])

    query_heads = grouped(queries.reshape(images, local_tokens, heads_here, head_size))
    key_heads = grouped(all_keys.reshape(images, seq_all, heads_here, head_size))
    value_heads = grouped(all_values.reshape(images, seq_all, heads_here, head_size))
    valid_groups = grouped(all_valid)
    attended, logsum = lax.map(attend_forward, (query_heads, key_heads, value_heads, valid_groups))
    heads_low = attended.reshape(rows_here, half_width)
    branch = (
        lax.psum(
            jnp.dot(heads_low, out_w, preferred_element_type=jnp.float32).astype(jnp.bfloat16), "tp"
        ).astype(jnp.float32)
        + vectors[4]
    )
    hidden = flat_rows + branch
    second, normal_two, inverse_two = norm_rows(hidden, vectors[5], vectors[6])
    second_low = second.astype(jnp.bfloat16)
    pre_active = jnp.dot(second_low, up_w, preferred_element_type=jnp.float32) + up_bias
    active_low = gelu_erf(pre_active).astype(jnp.bfloat16)
    mlp_sum = lax.psum(
        jnp.dot(active_low, down_w, preferred_element_type=jnp.float32).astype(jnp.bfloat16), "tp"
    ).astype(jnp.float32)
    output = (
        (hidden + mlp_sum + vectors[7])
        .astype(jnp.bfloat16)
        .reshape(images, local_tokens, model_width)
    )
    weight_rows = key_mask.astype(jnp.float32) * image_mask.astype(jnp.float32)[:, None]
    back = (cotangent.astype(jnp.float32) * weight_rows[:, :, None]).reshape(rows_here, model_width)
    back_low = back.astype(jnp.bfloat16)
    grad_active = jnp.einsum("td,fd->tf", back_low, down_w, preferred_element_type=jnp.float32)
    grad_pre = (grad_active * gelu_slope(pre_active)).astype(jnp.bfloat16)
    grad_down = jnp.einsum("tf,td->fd", active_low, back_low, preferred_element_type=jnp.float32)
    grad_up = jnp.einsum("td,tf->df", second_low, grad_pre, preferred_element_type=jnp.float32)
    grad_up_bias = jnp.sum(grad_pre.astype(jnp.float32), 0)
    grad_second = lax.psum(
        jnp.einsum("tf,df->td", grad_pre, up_w, preferred_element_type=jnp.float32).astype(
            jnp.bfloat16
        ),
        "tp",
    ).astype(jnp.float32)
    grad_hidden = back + norm_back(grad_second, normal_two, inverse_two, vectors[5])
    grad_branch = grad_hidden.astype(jnp.bfloat16)
    grad_out = jnp.einsum("tn,td->nd", heads_low, grad_branch, preferred_element_type=jnp.float32)
    grad_heads = jnp.einsum(
        "td,nd->tn", grad_branch, out_w, preferred_element_type=jnp.float32
    ).astype(jnp.bfloat16)
    grad_head_groups = grouped(grad_heads.reshape(images, local_tokens, heads_here, head_size))
    grad_queries, grad_keys, grad_values = lax.map(
        attend_back, (query_heads, key_heads, value_heads, valid_groups, logsum, grad_head_groups)
    )
    key_grads, value_grads = (
        lax.psum_scatter(
            grad_keys.reshape(images, seq_all, half_width).astype(jnp.bfloat16),
            "ctx",
            scatter_dimension=1,
            tiled=True,
        ).astype(jnp.float32),
        lax.psum_scatter(
            grad_values.reshape(images, seq_all, half_width).astype(jnp.bfloat16),
            "ctx",
            scatter_dimension=1,
            tiled=True,
        ).astype(jnp.float32),
    )
    grad_projected = jnp.stack(
        [
            grad_queries.reshape(rows_here, half_width),
            key_grads.reshape(rows_here, half_width).astype(jnp.bfloat16),
            value_grads.reshape(rows_here, half_width).astype(jnp.bfloat16),
        ],
        1,
    )
    grad_mix = jnp.einsum(
        "td,tcn->dcn", normed_low, grad_projected, preferred_element_type=jnp.float32
    )
    grad_normed = lax.psum(
        jnp.einsum("tcn,dcn->td", grad_projected, mix_w, preferred_element_type=jnp.float32).astype(
            jnp.bfloat16
        ),
        "tp",
    ).astype(jnp.float32)
    input_grad = (
        (grad_hidden + norm_back(grad_normed, normal_one, inverse_one, vectors[0]))
        .astype(jnp.bfloat16)
        .reshape(images, local_tokens, model_width)
    )
    projected_sums = jnp.sum(grad_projected.astype(jnp.float32), 0)
    vector_part = jnp.concatenate(
        [
            jnp.stack(
                [
                    jnp.sum(grad_normed * normal_one, 0) * tp_first,
                    jnp.sum(grad_normed, 0) * tp_first,
                    place_at(projected_sums[0], (model_width,), tp_index * half_width, 0),
                    place_at(projected_sums[2], (model_width,), tp_index * half_width, 0),
                    jnp.sum(grad_branch.astype(jnp.float32), 0) * tp_first,
                    jnp.sum(grad_second * normal_two, 0) * tp_first,
                    jnp.sum(grad_second, 0) * tp_first,
                    jnp.sum(back, 0) * tp_first,
                ]
            ),
            place_at(grad_up_bias, (FF,), tp_index * half_hidden, 0).reshape(-1, model_width),
        ],
        0,
    )
    shards = (
        lax.psum_scatter(grad_mix, "fsdp", scatter_dimension=0, tiled=True),
        lax.psum_scatter(grad_out, "fsdp", scatter_dimension=1, tiled=True),
        lax.psum_scatter(grad_up, "fsdp", scatter_dimension=0, tiled=True),
        lax.psum_scatter(grad_down, "fsdp", scatter_dimension=1, tiled=True),
    )
    sum_mix, sum_out, sum_up, sum_down = (
        lax.psum(shards[0].astype(jnp.bfloat16), "ctx").astype(jnp.float32),
        lax.psum(shards[1].astype(jnp.bfloat16), "ctx").astype(jnp.float32),
        lax.psum(shards[2].astype(jnp.bfloat16), "ctx").astype(jnp.float32),
        lax.psum(shards[3].astype(jnp.bfloat16), "ctx").astype(jnp.float32),
    )
    fsdp_start = fsdp_index * width_piece
    tp_width = tp_index * half_width
    tp_hidden = tp_index * half_hidden
    mix_square = sum_mix * sum_mix
    out_square = sum_out * sum_out
    up_square = sum_up * sum_up
    down_square = sum_down * sum_down
    scalar_part = (
        jnp.stack(
            [
                jnp.sum(qkv_weight * qkv_weight),
                jnp.sum(out_weight * out_weight),
                jnp.sum(up_weight * up_weight),
                jnp.sum(down_weight * down_weight),
                jnp.sum(row_qkv) * tp_first,
                jnp.sum(row_out) * fsdp_first,
                jnp.sum(row_up) * tp_first,
                jnp.sum(row_down) * fsdp_first,
            ]
        )
        * ctx_first
    )
    (
        vector_grad,
        rows_mix,
        cols_mix,
        rows_out,
        cols_out,
        rows_up,
        cols_up,
        rows_down,
        cols_down,
        scalar_sums,
    ) = lax.psum(
        (
            vector_part,
            place_at(jnp.sum(mix_square, (1, 2)), (model_width,), fsdp_start, 0) * ctx_first,
            place_at(jnp.sum(mix_square, 0), (3, model_width), tp_width, 1) * ctx_first,
            place_at(jnp.sum(out_square, 1), (model_width,), tp_width, 0) * ctx_first,
            place_at(jnp.sum(out_square, 0), (model_width,), fsdp_start, 0) * ctx_first,
            place_at(jnp.sum(up_square, 1), (model_width,), fsdp_start, 0) * ctx_first,
            place_at(jnp.sum(up_square, 0), (FF,), tp_hidden, 0) * ctx_first,
            place_at(jnp.sum(down_square, 1), (FF,), tp_hidden, 0) * ctx_first,
            place_at(jnp.sum(down_square, 0), (model_width,), fsdp_start, 0) * ctx_first,
            scalar_part,
        ),
        ("fsdp", "ctx", "tp"),
    )
    qkv_rows, qkv_cols_flat, mix_update = factor_local(
        sum_mix.reshape(width_piece, -1),
        row_qkv,
        col_qkv.reshape(-1),
        rows_mix,
        lax.dynamic_slice_in_dim(rows_mix, fsdp_start, width_piece),
        lax.dynamic_slice_in_dim(cols_mix, tp_width, half_width, 1).reshape(-1),
        model_width,
        3 * model_width,
        scalar_sums[4],
    )
    out_rows, out_cols, out_update = factor_local(
        sum_out,
        row_out,
        col_out,
        rows_out,
        lax.dynamic_slice_in_dim(rows_out, tp_width, half_width),
        lax.dynamic_slice_in_dim(cols_out, fsdp_start, width_piece),
        model_width,
        model_width,
        scalar_sums[5],
    )
    up_rows, up_cols, up_update = factor_local(
        sum_up,
        row_up,
        col_up,
        rows_up,
        lax.dynamic_slice_in_dim(rows_up, fsdp_start, width_piece),
        lax.dynamic_slice_in_dim(cols_up, tp_hidden, half_hidden),
        model_width,
        FF,
        scalar_sums[6],
    )
    down_rows, down_cols, down_update = factor_local(
        sum_down,
        row_down,
        col_down,
        rows_down,
        lax.dynamic_slice_in_dim(rows_down, tp_hidden, half_hidden),
        lax.dynamic_slice_in_dim(cols_down, fsdp_start, width_piece),
        FF,
        model_width,
        scalar_sums[7],
    )
    vector_moment = decay_rate * vector_moments + (1.0 - decay_rate) * vector_grad * vector_grad
    vector_step = vector_grad * lax.rsqrt(vector_moment)
    local_square = (
        jnp.sum(mix_update * mix_update)
        + jnp.sum(out_update * out_update)
        + jnp.sum(up_update * up_update)
        + jnp.sum(down_update * down_update)
    )
    global_square = lax.psum(local_square, ("fsdp", "tp")) + jnp.sum(vector_step * vector_step)
    param_count = 4 * model_width * model_width + 2 * model_width * FF + vectors.size
    shrink = 1.0 / jnp.maximum(1.0, jnp.sqrt(global_square / param_count) / clip_level)
    qkv_new = (
        qkv_weight
        - step_rate
        * jnp.sqrt(scalar_sums[0] / (3 * model_width * model_width))
        * mix_update.reshape(qkv_weight.shape)
        * shrink
    )
    out_new = (
        out_weight
        - step_rate * jnp.sqrt(scalar_sums[1] / (model_width * model_width)) * out_update * shrink
    )
    up_new = (
        up_weight - step_rate * jnp.sqrt(scalar_sums[2] / (model_width * FF)) * up_update * shrink
    )
    down_new = (
        down_weight
        - step_rate * jnp.sqrt(scalar_sums[3] / (model_width * FF)) * down_update * shrink
    )
    vector_new = vectors - step_rate * jnp.sqrt(jnp.mean(vectors * vectors)) * vector_step * shrink
    return (
        output,
        input_grad,
        sum_mix,
        sum_out,
        sum_up,
        sum_down,
        vector_grad,
        qkv_new,
        out_new,
        up_new,
        down_new,
        vector_new,
        qkv_new.astype(jnp.bfloat16),
        out_new.astype(jnp.bfloat16),
        up_new.astype(jnp.bfloat16),
        down_new.astype(jnp.bfloat16),
        qkv_rows,
        qkv_cols_flat.reshape(3, half_width),
        out_rows,
        out_cols,
        up_rows,
        up_cols,
        down_rows,
        down_cols,
        vector_moment,
    )


def solution(mesh):
    placed = (
        P("fsdp", "ctx", None),
        P("fsdp", "ctx", None),
        P("fsdp", "ctx"),
        P("fsdp"),
        P("fsdp", None, "tp"),
        P("tp", "fsdp"),
        P("fsdp", "tp"),
        P("tp", "fsdp"),
        P(),
        P("fsdp"),
        P(None, "tp"),
        P("tp"),
        P("fsdp"),
        P("fsdp"),
        P("tp"),
        P("tp"),
        P("fsdp"),
        P(),
    )
    return jax.shard_map(
        body,
        mesh=mesh,
        in_specs=placed,
        out_specs=(
            P("fsdp", "ctx", None),
            P("fsdp", "ctx", None),
            P("fsdp", None, "tp"),
            P("tp", "fsdp"),
            P("fsdp", "tp"),
            P("tp", "fsdp"),
            P(),
            P("fsdp", None, "tp"),
            P("tp", "fsdp"),
            P("fsdp", "tp"),
            P("tp", "fsdp"),
            P(),
            P("fsdp", None, "tp"),
            P("tp", "fsdp"),
            P("fsdp", "tp"),
            P("tp", "fsdp"),
            P("fsdp"),
            P(None, "tp"),
            P("tp"),
            P("fsdp"),
            P("fsdp"),
            P("tp"),
            P("tp"),
            P("fsdp"),
            P(),
        ),
        check_vma=False,
    )
```

profile of v0, /device:TPU:0, one launch (start us, length us, event | category | flops | bytes accessed | tf_op | source)
XLA Modules:
  0.0 1435.3 jit_solution(17958598318135853181)
XLA Ops:
  23.9 50.1 %all-gather.8.cloned.1.call-done = bf16[1024,3,512]{2,0,1:T(8,128)(2,1)} async-done(((bf16[128,3,512]{2,0,1:T(8,128)(2,1)}), bf16[1024,3,512]{2,0,1:T(8,128)(2,1)}) %all-gather.8.cloned.1.call-update) | async-done | bytes 3145744 | tf_op jit(solution)/shard_map/all_gather | solution.py:140
  111.4 9.9 all-gather.12.cloned.1.call-done
  125.8 33.4 %all-gather.10.cloned.1.call-done = bf16[4,580,512]{2,0,1:T(4,128)(2,1)} async-done(((bf16[4,290,512]{2,0,1:T(4,128)(2,1)}), bf16[4,580,512]{2,0,1:T(4,128)(2,1)}) %all-gather.10.cloned.1.call-update) | async-done | bytes 2375696 | tf_op jit(solution)/shard_map/all_gather | solution.py:161
  164.7 25.8 %while.26 = (s32[]{:T(128)}, bf16[2,2,290,8,64]{2,1,0,4,3:T(2,128)(2,1)}, f32[2,2,8,290]{3,2,1,0:T(8,128)S(1)}, bf16[2,2,580,8,64]{2,4,3,1,0:T(8,128)(2,1)}, bf1...) while((s32[]{:T(128)}, ...), condition=%wide.region_5.6_spmd, body=%wide.region_2.5_spmd.sunk | while | flops 721535104 | bytes 58423392 | solution.py:175
  234.8 69.1 %all-gather.16.cloned.1.call-done = bf16[1024,2048]{1,0:T(8,128)(2,1)} async-done(((bf16[128,2048]{1,0:T(8,128)(2,1)}), bf16[1024,2048]{1,0:T(8,128)(2,1)}) %all-gather.16.cloned.1.call-update) | async-done | bytes 4194320 | tf_op jit(solution)/shard_map/all_gather | solution.py:142
  303.8 12.4 multiply_convert_fusion.2
  316.2 63.8 %all-gather.18.cloned.1.call-done = bf16[2048,1024]{1,0:T(8,128)(2,1)} async-done(((bf16[2048,128]{1,0:T(8,128)(2,1)}), bf16[2048,1024]{1,0:T(8,128)(2,1)}) %all-gather.18.cloned.1.call-update) | async-done | bytes 4194320 | tf_op jit(solution)/shard_map/all_gather | solution.py:143
  380.0 12.3 convert_reduce_fusion
  401.0 19.9 %all-reduce.15.cloned.1.call-done = bf16[1160,1024]{1,0:T(8,128)(2,1)} async-done(((bf16[1160,1024]{1,0:T(8,128)(2,1)}), bf16[1160,1024]{1,0:T(8,128)(2,1)}) %all-reduce.15.cloned.1.call-update) | async-done | bytes 2375696 | tf_op jit(solution)/shard_map/psum | solution.py:204
  444.5 53.2 %while.27 = (s32[]{:T(128)}, bf16[2,2,290,8,64]{2,4,3,1,0:T(8,128)(2,1)}, bf16[2,2,580,8,64]{2,4,3,1,0:T(8,128)(2,1)}, bf16[2,2,580,8,64]{2,4,3,1,0:T(8,128)(2,1...) while((s32[]{:T(128)}, ...), condition=%wide.region_15.16_spmd, body=%wide.region_13.15_spmd.sunk | while | flops 1763920384 | bytes 145100528 | solution.py:217
  515.0 9.5 convolution_convert_fusion.1
  532.6 96.0 %all-reduce.23.cloned.1.call-done = (bf16[4,580,512]{2,0,1:T(4,128)(2,1)}, bf16[4,580,512]{2,0,1:T(4,128)(2,1)}) async-done(((bf16[4,580,512]{2,0,1:T(4,128)(2,1)}, bf16[4,580,512]{2,0,1:T(4,128)(2,1)}), (bf16[4,580,512]{2,0,1:T(4,128)(2,1)}, bf16[4,580,512]{2,0,1:T(4,128)(2,1)})) %all-reduce.23.cloned.1.call-update) | async-done | bytes 4751376
  637.7 8.5 bitcast_convert_fusion
  646.2 11.1 fusion.76
  658.0 11.6 fusion.88
  670.3 10.9 fusion.84
  692.0 8.8 reduce-scatter.7.cloned.1.call-done
  705.0 27.5 %all-reduce.19.cloned.1.call-done = (bf16[1160,1024]{1,0:T(8,128)(2,1)}, bf16[1160,1024]{1,0:T(8,128)(2,1)}) async-done(((bf16[1160,1024]{1,0:T(8,128)(2,1)}, bf16[1160,1024]{1,0:T(8,128)(2,1)}), (bf16[1160,1024]{1,0:T(8,128)(2,1)}, bf16[1160,1024]{1,0:T(8,128)(2,1)})) %all-reduce.19.cloned.1.call-update) | async-done | bytes 4751376 | tf_op jit(solution)/shard_map/psum | solution.py:188
  737.3 149.3 %reduce-scatter.11.cloned.1.call-done = f32[2048,128]{1,0:T(8,128)} async-done(((f32[2048,1024]{1,0:T(8,128)}), f32[2048,128]{1,0:T(8,128)}) %reduce-scatter.11.cloned.1.call-update) | async-done | bytes 1048592 | tf_op jit(solution)/shard_map/reduce_scatter | solution.py:279
  888.7 150.0 %reduce-scatter.9.cloned.1.call-done = f32[128,2048]{1,0:T(8,128)} async-done(((f32[1024,2048]{1,0:T(8,128)}), f32[128,2048]{1,0:T(8,128)}) %reduce-scatter.9.cloned.1.call-update) | async-done | bytes 1048592 | tf_op jit(solution)/shard_map/reduce_scatter | solution.py:278
  1040.8 118.8 %reduce-scatter.5.cloned.1.call-done = f32[128,3,512]{2,0,1:T(8,128)} async-done(((f32[1024,3,512]{2,0,1:T(8,128)}), f32[128,3,512]{2,0,1:T(8,128)}) %reduce-scatter.5.cloned.1.call-update) | async-done | bytes 786448 | tf_op jit(solution)/shard_map/reduce_scatter | solution.py:276
  1168.8 44.9 %all-reduce.21.cloned.1.call-done = (bf16[128,3,512]{2,0,1:T(8,128)(2,1)}, bf16[512,128]{1,0:T(8,128)(2,1)}, bf16[128,2048]{1,0:T(8,128)(2,1)}, bf16[2048,128]{1,0:T(8,128)(2,1)}) async-done(((bf16[128,3,512]{2,0,1:T(8,128)(2,1)}, bf16[512,128]{1,0:T(8,128)(2,1)}, bf16[128,2048]{1,0:T(8,128)(2,1)}, bf16[2048,128]{1,0:T(8,128)(2,1)}), (bf16[128,3,512]{2,0,1:T(8,128)(2,1)}, bf16[512,128]{1,0:T(8,128)(2,1)}, ...) | async-done | bytes 1572880 | tf_op jit(solution)/shard_map/psum | solution.py:282
  1242.8 110.3 %all-reduce.17.cloned.1.call-done = (f32[12,1024]{1,0:T(8,128)}, f32[8]{0:T(128)}, f32[1024]{0:T(1024)}, f32[3,1024]{1,0:T(4,128)}, f32[1024]{0:T(1024)}, /*inde...) async-done(((f32[12,1024]{1,0:T(8,128)}, f32[8]{0:T(128)}, f32[1024]{0:T(1024)}, f32[3,1024]{1,0:T(4,128)}, f32[1024]{0:T(1024)}, ...) | async-done | bytes 114736 | tf_op jit(solution)/shard_map/psum | solution.py:320
  1381.2 34.2 %psum.151 = f32[]{:T(128)} all-reduce(f32[]{:T(128)S(6)} %add.306), channel_id=1, replica_groups=mesh['fsdp'=8,'ctx'=2,'tp'=2] {'fsdp','tp'}, use_global_device_ids=true, to_apply=%region_71.72 | all-reduce | flops 1 | bytes 8 | tf_op jit(solution)/shard_map/psum | solution.py:387
  (387 shorter events, 341.3 us)
Async XLA Ops:
  7.2 66.8 %all-gather.8.cloned.1.call-start = ((), (), s32[]{:S(2)}) async-start(), calls=%async_computation.4 | async-start | bytes 3538944 | tf_op jit(solution)/shard_map/all_gather | solution.py:140
  10.3 111.0 %all-gather.12.cloned.1.call-start = ((), (), s32[]{:S(2)}) async-start(), calls=%async_computation.6 | async-start | bytes 3563520 | tf_op jit(solution)/shard_map/all_gather | solution.py:160
  86.3 72.9 %all-gather.10.cloned.1.call-start = ((), (), s32[]{:S(2)}) async-start(), calls=%async_computation.5 | async-start | bytes 3563520 | tf_op jit(solution)/shard_map/all_gather | solution.py:161
  95.7 106.3 %all-gather.14.cloned.1.call-start = ((), (), s32[]{:S(2)}) async-start(), calls=%async_computation.7 | async-start | bytes 1179648 | tf_op jit(solution)/shard_map/all_gather | solution.py:141
  97.1 131.0 %all-reduce.13.cloned.1.call-start = ((), (), s32[]{:S(2)}) async-start(), calls=%async_computation.8 | async-start | bytes 4751360 | tf_op jit(solution)/shard_map/psum | solution.py:178
  206.5 97.3 %all-gather.16.cloned.1.call-start = ((), (), s32[]{:S(2)}) async-start(), calls=%async_computation.9 | async-start | bytes 4718592 | tf_op jit(solution)/shard_map/all_gather | solution.py:142
  209.8 170.2 %all-gather.18.cloned.1.call-start = ((), (), s32[]{:S(2)}) async-start(), calls=%async_computation.10 | async-start | bytes 4718592 | tf_op jit(solution)/shard_map/all_gather | solution.py:143
  213.6 207.3 %all-reduce.15.cloned.1.call-start = ((), (), s32[]{:S(2)}) async-start(), calls=%async_computation.11 | async-start | bytes 4751360 | tf_op jit(solution)/shard_map/psum | solution.py:204
  231.9 71.9 %copy-start.40 = (f32[1,1024]{1,0:T(1,128)S(1)}, f32[1,1024]{1,0:T(1,128)}, u32[]{:S(2)}) copy-start(f32[1,1024]{1,0:T(1,128)} %get-tuple-element.471) | copy-start | bytes 12292
  232.0 194.4 %copy-start.29 = (f32[1160]{0:T(1024)}, f32[1160]{0:T(1024)S(1)}, u32[]{:S(2)}) copy-start(f32[1160]{0:T(1024)S(1)} %broadcast_multiply_fusion.8) | copy-start | bytes 13924
  234.7 191.6 %copy-start.38 = (f32[1160]{0:T(1024)}, f32[1160]{0:T(1024)S(1)}, u32[]{:S(2)}) copy-start(f32[1160]{0:T(1024)S(1)} %add_rsqrt_fusion.1) | copy-start | bytes 13924
  400.9 227.7 %all-reduce.23.cloned.1.call-start = ((), (), s32[]{:S(2)}) async-start(), calls=%async_computation.19 | async-start | bytes 9502720
  507.1 193.7 %reduce-scatter.7.cloned.1.call-start = ((), (), s32[]{:S(2)}) async-start(), calls=%async_computation.13 | async-start | bytes 2359296 | tf_op jit(solution)/shard_map/reduce_scatter | solution.py:277
  513.7 218.9 %all-reduce.19.cloned.1.call-start = ((), (), s32[]{:S(2)}) async-start(), calls=%async_computation.17 | async-start | bytes 9502720 | tf_op jit(solution)/shard_map/psum | solution.py:188
  646.2 240.4 %reduce-scatter.11.cloned.1.call-start = ((), (), s32[]{:S(2)}) async-start(), calls=%async_computation.15 | async-start | bytes 9437184 | tf_op jit(solution)/shard_map/reduce_scatter | solution.py:279
  657.3 381.4 %reduce-scatter.9.cloned.1.call-start = ((), (), s32[]{:S(2)}) async-start(), calls=%async_computation.14 | async-start | bytes 9437184 | tf_op jit(solution)/shard_map/reduce_scatter | solution.py:278
  669.6 489.9 %reduce-scatter.5.cloned.1.call-start = ((), (), s32[]{:S(2)}) async-start(), calls=%async_computation.12 | async-start | bytes 7077888 | tf_op jit(solution)/shard_map/reduce_scatter | solution.py:276
  681.3 532.3 %all-reduce.21.cloned.1.call-start = ((), (), s32[]{:S(2)}) async-start(), calls=%async_computation.18 | async-start | bytes 3145728 | tf_op jit(solution)/shard_map/psum | solution.py:282
  737.2 425.6 %copy-start.8 = (bf16[1160,1024]{1,0:T(8,128)(2,1)S(1)}, bf16[1160,1024]{1,0:T(8,128)(2,1)}, u32[]{:S(2)}) copy-start(bf16[1160,1024]{1,0:T(8,128)(2,1)} %get-tuple-element.428) | copy-start | bytes 7127044
  1161.5 191.6 %all-reduce.17.cloned.1.call-start = ((), (), s32[]{:S(2)}) async-start(), calls=%async_computation.16 | async-start | bytes 271360 | tf_op jit(solution)/shard_map/psum | solution.py:320
  1221.5 204.1 %copy-start.10 = (f32[128,2048]{1,0:T(8,128)}, f32[128,2048]{1,0:T(8,128)S(1)}, u32[]{:S(2)}) copy-start(f32[128,2048]{1,0:T(8,128)S(1)} %get-tuple-element.670) | copy-start | bytes 3145732
  1237.3 132.2 %copy-start.53 = (f32[3,512]{1,0:T(4,128)S(1)}, f32[3,512]{1,0:T(4,128)}, u32[]{:S(2)}) copy-start(f32[3,512]{1,0:T(4,128)} %param.32) | copy-start | bytes 18436
  1242.8 177.5 %copy-start.12 = (f32[128,3,512]{2,0,1:T(8,128)S(1)}, f32[128,3,512]{2,0,1:T(8,128)}, u32[]{:S(2)}) copy-start(f32[128,3,512]{2,0,1:T(8,128)} %get-tuple-element.668) | copy-start | bytes 2359300
  1242.8 179.9 %copy-start.11 = (f32[2048,128]{1,0:T(8,128)S(1)}, f32[2048,128]{1,0:T(8,128)}, u32[]{:S(2)}) copy-start(f32[2048,128]{1,0:T(8,128)} %get-tuple-element.671) | copy-start | bytes 3145732
  (73 other events, 1109.2 us)
Sparse Core Ops, SparseCore 0:
  10.8 63.2 all-gather.7
  86.4 34.9 all-gather.11
  122.9 36.2 all-gather.9
  161.7 40.2 all-gather.13
  206.6 19.7 all-reduce.12
  229.2 74.5 all-gather.15
  306.6 73.3 all-gather.17
  401.1 19.7 all-reduce.14
  507.2 121.4 all-reduce.22
  632.5 68.2 reduce-scatter.6
  704.1 28.3 all-reduce.18
  736.0 150.5 reduce-scatter.10
  890.7 147.9 reduce-scatter.8
  1042.2 117.3 reduce-scatter.4
  1162.5 51.1 all-reduce.20
  1227.2 125.8 all-reduce.16
where the time goes:
time: 1440 us
  waiting for transfers between devices  959 us (67%)
  matrix products  153 us (11%)
  local copies, waits for them, and re-layouts  130 us (9%)
  other arithmetic  122 us (8%)
  blocking collectives  39 us (3%)
  between operations  31.1 us (2%)
    reduce_scatter x1, waiting for transfers between devices, body(): lax.psum_scatter(grad_up, 'fsdp', scatter_dimension=0, tiled=True)  150 us
    reduce_scatter x1, waiting for transfers between devices, body(): lax.psum_scatter(grad_down, 'fsdp', scatter_dimension=1, tiled=True)  149 us
    reduce_scatter x1, waiting for transfers between devices, body(): lax.psum_scatter(grad_mix, 'fsdp', scatter_dimension=0, tiled=True)  119 us
    psum x1, waiting for transfers between devices, body(): lax.psum((vector_part, place_at(jnp.sum(mix_square, (1, 2)), (model_width...  110 us
    unnamed x17, waiting for transfers between devices  96.3 us
    all_gather x1, waiting for transfers between devices, body(): lax.all_gather(up_weight.astype(jnp.bfloat16), 'fsdp', axis=0, tiled=True)  69.1 us
    all_gather x1, waiting for transfers between devices, body(): lax.all_gather(down_weight.astype(jnp.bfloat16), 'fsdp', axis=1, tiled=True)  63.8 us
    all_gather x1, waiting for transfers between devices, body(): lax.all_gather(qkv_weight.astype(jnp.bfloat16), 'fsdp', axis=0, tiled=True)  50.1 us
  transfers between devices with their start and end apart: 16, of which 15 were waited for; matrix products, arithmetic and copies ran while one was open for 16% of the time, Pallas kernels for 0%

commit v1 on v0

--- a/solution.py
+++ b/solution.py
@@ -1,6 +1,8 @@
 import jax
 import jax.numpy as jnp
 from jax import lax
+from jax.experimental import pallas as pl
+from jax.experimental.pallas import tpu as pltpu
 from jax.sharding import PartitionSpec as P
 
 HD = 64
@@ -435,6 +437,1176 @@
     )
 
 
+MESH = pl.DeviceIdType.MESH
+LANES = 128
+SLOTS = 320
+ROWS = 2 * SLOTS
+WIDE = 512
+CHUNKS = 12
+PAIRS = 8
+MIB = 1024 * 1024
+
+
+def place():
+    shard = lax.axis_index("fsdp")
+    return (lax.div(shard, 2), lax.rem(shard, 2), lax.axis_index("ctx"), lax.axis_index("tp"))
+
+
+def peers_of(z, y, x, c):
+    line = [(lax.rem(z + step, 4) * 2 + y, x, c) for step in (1, 2, 3)]
+    return (line, (z * 2 + 1 - y, x, c), (z * 2 + y, 1 - x, c), (z * 2 + y, x, 1 - c))
+
+
+def greet(peers):
+    barrier = pltpu.get_barrier_semaphore()
+    for peer in peers:
+        pl.semaphore_signal(barrier, inc=1, device_id=peer, device_id_type=MESH)
+    pl.semaphore_wait(barrier, len(peers))
+
+
+def remote(src, dst, send, recv, peer):
+    return pltpu.make_async_remote_copy(
+        src_ref=src, dst_ref=dst, send_sem=send, recv_sem=recv, device_id=peer, device_id_type=MESH
+    )
+
+
+def nn(left, right):
+    return lax.dot_general(left, right, (((1,), (0,)), ((), ())), preferred_element_type=jnp.float32)
+
+
+def nt(left, right):
+    return lax.dot_general(left, right, (((1,), (1,)), ((), ())), preferred_element_type=jnp.float32)
+
+
+def aligned(start, size, unit):
+    if isinstance(start, int):
+        return pl.ds(start, size)
+    return pl.ds(pl.multiple_of(start, unit), size)
+
+
+def columns(start, size):
+    return aligned(start, size, LANES)
+
+
+def slots_valid(counts, axis):
+    shape = (1, ROWS) if axis else (ROWS, 1)
+    slot = lax.broadcasted_iota(jnp.int32, shape, axis)
+    first = counts[0, 0:1, 0:1].astype(jnp.int32)
+    second = counts[1, 0:1, 0:1].astype(jnp.int32)
+    return ((slot < SLOTS) & (slot < first)) | ((slot >= SLOTS) & (slot - SLOTS < second))
+
+
+def square_sum(ref):
+    flat = ref if len(ref.shape) == 2 else ref.reshape(ref.shape[0] * ref.shape[1], ref.shape[2])
+    step = flat.shape[0] // 8
+
+    def add(at, total):
+        values = flat[pl.ds(pl.multiple_of(at * step, step), step), :]
+        return total + jnp.sum(values * values, 0, keepdims=True)
+
+    total = lax.fori_loop(0, 8, add, jnp.zeros((1, flat.shape[1]), jnp.float32))
+    return jnp.sum(total, 1, keepdims=True)
+
+
+def front_body(
+    x_in, b_in, n_in, mix_w, out_w, up_w, down_w, vectors,
+    kept, b_out, x_out, n_out, qkv, heads, hidden, second, squares,
+    normed, w, wo,
+    local, in_s, in_r, zs, zr, ys, yr, xs, xr, cs, cr, ws,
+):
+    z, y, x, c = place()
+    line, y_peer, x_peer, c_peer = peers_of(z, y, x, c)
+    own = []
+    mine, theirs = 2 * x + c, 2 * (1 - x) + c
+    pairs = ((x_in, x_out), (n_in, n_out), (b_in, b_out))
+    for at, (src, dst) in enumerate(pairs):
+        own.append(pltpu.make_async_copy(src.at[mine], dst.at[x], local.at[at]))
+    for copy in own:
+        copy.start()
+    low = jnp.bfloat16
+    for k in range(4):
+        lanes = pl.ds(k * LANES, LANES)
+        for part in range(3):
+            w[k, c, z, y, :, pl.ds(part * LANES, LANES)] = mix_w[part, :, lanes].astype(low)
+        w[k, c, z, y, :, pl.ds(3 * LANES, LANES)] = out_w[lanes, :].T.astype(low)
+        w[4 + 2 * k, c, z, y] = up_w[:, pl.ds(k * WIDE, WIDE)].astype(low)
+        for part in range(4):
+            rows = pl.ds(k * WIDE + part * LANES, LANES)
+            w[5 + 2 * k, c, z, y, :, pl.ds(part * LANES, LANES)] = down_w[rows, :].T.astype(low)
+    greet(line + [y_peer, x_peer, c_peer])
+    swaps = [
+        remote(src.at[theirs], dst.at[x], in_s.at[at], in_r.at[at], x_peer)
+        for at, (src, dst) in enumerate(pairs)
+    ]
+
+    def share(odd):
+        size = 80 if odd else 96
+        return aligned(x * (128 - size), size, 16), aligned(x * size, 128 - size, 16)
+
+    def z_copies(k, odd):
+        block = w.at[k, c, z, y, share(odd)[0]]
+        return [remote(block, block, zs.at[k, at], zr.at[k, at], peer) for at, peer in enumerate(line)]
+
+    def y_copies(k, odd):
+        rows = share(odd)[0]
+        blocks = [w.at[k, c, pl.ds(2 * at, 2), y, rows] for at in range(2)]
+        return [remote(block, block, ys.at[k, at], yr.at[k, at], y_peer) for at, block in enumerate(blocks)]
+
+    def x_copies(k, odd):
+        rows = share(odd)[1]
+        blocks = [w.at[k, c, at, :, rows] for at in range(4)]
+        return [remote(block, block, xs.at[k, at], xr.at[k, at], x_peer) for at, block in enumerate(blocks)]
+
+    def c_copies(k):
+        blocks = [w.at[k, c, at] for at in range(4)]
+        return [remote(block, block, cs.at[k, at], cr.at[k, at], c_peer) for at, block in enumerate(blocks)]
+
+    def keep(k):
+        return pltpu.make_async_copy(w.at[k], kept.at[k], ws.at[k])
+
+    def start(copies):
+        for copy in copies:
+            copy.start()
+
+    def arrive(copies):
+        for copy in copies:
+            copy.wait_recv()
+
+    ahead = 2
+
+    def within(k):
+        return not isinstance(k, int) or 0 <= k < CHUNKS
+
+    def link_step(t, odd):
+        if within(t):
+            arrive(z_copies(t, odd))
+            start(y_copies(t, odd))
+        if isinstance(t, int):
+            if within(t + ahead):
+                start(z_copies(t + ahead, odd))
+        else:
+
+            @pl.when(t + ahead < CHUNKS)
+            def _():
+                start(z_copies(t + ahead, odd))
+
+        if within(t - 2):
+            arrive(y_copies(t - 2, odd))
+            start(x_copies(t - 2, odd))
+        if within(t - 4):
+            arrive(x_copies(t - 4, odd))
+            start(c_copies(t - 4))
+        if within(t - 6):
+            arrive(c_copies(t - 6))
+            keep(t - 6).start()
+
+    swaps[0].start()
+    swaps[1].start()
+    for t in range(ahead):
+        start(z_copies(t, t % 2 == 1))
+    swaps[2].start()
+    own[0].wait()
+    own[1].wait()
+
+    def norm_first(half):
+        @pl.loop(0, SLOTS // 64)
+        def _(at):
+            rows = pl.ds(pl.multiple_of(at * 64, 64), 64)
+            result, _, _ = norm_rows(
+                x_out[half, rows, :].astype(jnp.float32), vectors[0:1, :], vectors[1:2, :]
+            )
+            normed[half, rows, :] = result.astype(jnp.bfloat16)
+
+    norm_first(x)
+    for m, ref in enumerate((mix_w, out_w, up_w, down_w)):
+        squares[pl.ds(m, 1), :] = jnp.broadcast_to(square_sum(ref), (1, LANES))
+    link_step(0, False)
+    swaps[0].wait_recv()
+    swaps[1].wait_recv()
+    norm_first(1 - x)
+    for t in range(1, 7):
+        link_step(t, t % 2 == 1)
+    valid = slots_valid(n_out, 1)
+    lane = lax.broadcasted_iota(jnp.int32, (1, LANES), 1)
+
+    def pair_task(side, k):
+        pair = side * 4 + k
+        weights = w[k, side].reshape(1024, WIDE)
+        wo[:, columns(pair * LANES, LANES)] = weights[:, 3 * LANES :]
+        weights = weights[:, : 3 * LANES]
+        q_bias = vectors[2:3, columns(pair * LANES, LANES)]
+        v_bias = vectors[3:4, columns(pair * LANES, LANES)]
+        bias = jnp.concatenate([q_bias, jnp.zeros_like(q_bias), v_bias], 1)
+        for half in range(2):
+            qkv[pair, pl.ds(half * SLOTS, SLOTS), :] = (nn(normed[half], weights) + bias).astype(
+                jnp.bfloat16
+            )
+
+        @pl.loop(0, 2)
+        def _(half):
+            rows = pl.ds(pl.multiple_of(half * SLOTS, SLOTS), SLOTS)
+            queries = qkv[pair, rows, pl.ds(0, LANES)] * jnp.bfloat16(0.125)
+            keys = qkv[pair, :, pl.ds(LANES, LANES)]
+            values = qkv[pair, :, pl.ds(2 * LANES, LANES)]
+            results = []
+            for at in range(2):
+                here = (lane < HD) if at == 0 else (lane >= HD)
+                scores = nt(jnp.where(here, queries, jnp.zeros_like(queries)), keys)
+                scores = jnp.where(valid, scores, -1000000000.0)
+                top = jnp.max(scores, 1, keepdims=True)
+                exponent = jnp.exp(scores - top)
+                attention = exponent * (1.0 / jnp.sum(exponent, 1, keepdims=True))
+                results.append(nn(attention.astype(jnp.bfloat16), values))
+            heads[rows, columns(pair * LANES, LANES)] = jnp.where(
+                lane < HD, results[0], results[1]
+            ).astype(jnp.bfloat16)
+
+    for k in range(4):
+        pair_task(0, k)
+        link_step(2 * k + 7, True)
+        pair_task(1, k)
+        link_step(2 * k + 8, False)
+
+    for tile in range(4):
+        for half in range(2):
+            rows = pl.ds(half * SLOTS, SLOTS)
+            cols = pl.ds(tile * 256, 256)
+            branch = nt(heads[rows, :], wo[cols, :])
+            hidden[rows, cols] = x_out[half, :, cols].astype(jnp.float32) + (branch + vectors[4:5, cols])
+        if tile < 3:
+            link_step(15 + tile, tile != 1)
+
+    @pl.loop(0, ROWS // 64)
+    def _(at):
+        rows = pl.ds(pl.multiple_of(at * 64, 64), 64)
+        result, _, _ = norm_rows(hidden[rows, :], vectors[5:6, :], vectors[6:7, :])
+        second[rows, :] = result.astype(jnp.bfloat16)
+
+    own[2].wait()
+    for k in range(CHUNKS):
+        keep(k).wait()
+    swaps[2].wait_recv()
+    for swap in swaps:
+        swap.wait_send()
+
+    @pl.loop(0, CHUNKS // 2)
+    def _(at):
+        for odd in (False, True):
+            k = 2 * at + int(odd)
+            for copy in z_copies(k, odd) + y_copies(k, odd) + x_copies(k, odd) + c_copies(k):
+                copy.wait_send()
+
+
+def front_all(x_in, b_in, n_in, weights, vectors):
+    dma = pltpu.SemaphoreType.DMA
+    low, full = jnp.bfloat16, jnp.float32
+    anywhere = pl.BlockSpec(memory_space=pl.ANY)
+    in_vmem = pl.BlockSpec(memory_space=pltpu.VMEM)
+    shape = jax.ShapeDtypeStruct
+    width = x_in.shape[2]
+    return pl.pallas_call(
+        front_body,
+        out_shape=(
+            shape((CHUNKS, 2, 4, 2, 128, WIDE), low),
+            shape((2, SLOTS, width), low),
+            shape((2, SLOTS, width), low),
+            shape((2, 8, LANES), full),
+            shape((PAIRS, ROWS, 3 * LANES), low),
+            shape((ROWS, width), low),
+            shape((ROWS, width), full),
+            shape((ROWS, width), low),
+            shape((8, LANES), full),
+        ),
+        in_specs=[anywhere] * 3 + [in_vmem] * 5,
+        out_specs=(anywhere, anywhere) + (in_vmem,) * 7,
+        scratch_shapes=[
+            pltpu.VMEM((2, SLOTS, width), low),
+            pltpu.VMEM((CHUNKS, 2, 4, 2, 128, WIDE), low),
+            pltpu.VMEM((1024, 1024), low),
+            dma((3,)), dma((3,)), dma((3,)), dma((CHUNKS, 3)), dma((CHUNKS, 3)),
+            dma((CHUNKS, 2)), dma((CHUNKS, 2)), dma((CHUNKS, 4)), dma((CHUNKS, 4)), dma((CHUNKS, 4)), dma((CHUNKS, 4)),
+            dma((CHUNKS,)),
+        ],
+        compiler_params=pltpu.CompilerParams(
+            collective_id=0, has_side_effects=True, vmem_limit_bytes=58 * MIB
+        ),
+    )(x_in, b_in, n_in, *weights, vectors)
+
+
+def add_into(held, index, arrived, from_index):
+    held[index] = (
+        held[index].astype(jnp.float32) + arrived[from_index].astype(jnp.float32)
+    ).astype(jnp.bfloat16)
+
+
+class Scatter:
+    def __init__(self, crosswise, refs):
+        self.crosswise = crosswise
+        self.where = place()
+        self.line, self.y_peer, self.x_peer, self.c_peer = peers_of(*self.where)
+        x = self.where[2]
+        self.near = aligned(x * 64, 64, 64)
+        self.far = aligned((1 - x) * 64, 64, 64)
+        self.slot = [sum(k == crosswise[at] for k in crosswise[:at]) for at in range(len(crosswise))]
+        (
+            self.g, self.cb, self.xa, self.ya, self.za, self.fa, self.yb, self.zb, self.xb, self.stage,
+            self.cs, self.cr, self.s1s, self.s1r, self.s2s, self.s2r, self.s3s, self.s3r, self.s4s, self.s4r,
+            self.out_sem, self.free,
+        ) = refs[:22]
+        self.totals = refs[22:]
+        self.waited = set()
+
+    def hops(self, stage, q):
+        z, y, x, c = self.where
+        at, own = self.slot[q], self.g.at[q % 8]
+        if stage == 0:
+            return [
+                remote(self.g.at[8 + q % 4], self.cb.at[q % 4], self.cs.at[q], self.cr.at[q], self.c_peer)
+            ]
+        first, third = (self.s1s.at[q], self.s1r.at[q]), (self.s4s.at[q], self.s4r.at[q])
+        second, last = (self.s2s.at[q], self.s2r.at[q]), (self.s3s.at[q], self.s3r.at[q])
+        ahead = [lax.rem(z + d + 1, 4) for d in range(3)]
+        if self.crosswise[q]:
+            near = self.near
+            if stage == 1:
+                return [remote(own.at[:, :, self.far], self.xa.at[at], *first, self.x_peer)]
+            if stage == 2:
+                return [
+                    remote(own.at[:, 1 - y, near], self.ya.at[at], second[0].at[0], second[1].at[0], self.y_peer)
+                ]
+            if stage == 3:
+                return [
+                    remote(own.at[to, y, near], self.za.at[at, d], last[0].at[d], last[1].at[d], peer)
+                    for d, (to, peer) in enumerate(zip(ahead, self.line))
+                ]
+            return [remote(own.at[z, y, near], self.fa.at[at], *third, self.x_peer)]
+        if stage == 1:
+            return [remote(own.at[:, 1 - y], self.yb.at[at], *first, self.y_peer)]
+        if stage == 2:
+            return [
+                remote(own.at[to, y], self.zb.at[at, d], second[0].at[d], second[1].at[d], peer)
+                for d, (to, peer) in enumerate(zip(ahead, self.line))
+            ]
+        if stage == 3:
+            return [remote(own.at[z, y], self.xb.at[at], last[0].at[0], last[1].at[0], self.x_peer)]
+        return []
+
+    def start(self, stage, q):
+        for copy in self.hops(stage, q):
+            copy.start()
+
+    def arrive(self, stage, q):
+        for copy in self.hops(stage, q):
+            copy.wait_recv()
+
+    def sent(self, q, stages):
+        for stage in stages:
+            self.waited.add((stage, q))
+            for copy in self.hops(stage, q):
+                copy.wait_send()
+
+    def begin(self, q):
+        if q >= 4:
+            pl.semaphore_wait(self.free.at[q % 4], 1)
+        self.start(0, q)
+
+    def one(self, q):
+        self.arrive(0, q)
+
+        @pl.loop(0, 8)
+        def _(block):
+            zi, yi = lax.div(block, 2), lax.rem(block, 2)
+            add_into(self.g, (q % 8, zi, yi), self.cb, (q % 4, zi, yi))
+
+        if q < 8:
+            pl.semaphore_signal(
+                self.free.at[q % 4], inc=1, device_id=self.c_peer, device_id_type=MESH
+            )
+
+        self.start(1, q)
+
+    def two(self, q):
+        y, at = self.where[1], self.slot[q]
+        self.arrive(1, q)
+        if self.crosswise[q]:
+
+            @pl.loop(0, 8)
+            def _(block):
+                zi, yi = lax.div(block, 2), lax.rem(block, 2)
+                add_into(self.g, (q % 8, zi, yi, self.near), self.xa, (at, zi, yi))
+
+        else:
+
+            @pl.loop(0, 4)
+            def _(zi):
+                add_into(self.g, (q % 8, zi, y), self.yb, (at, zi))
+
+        self.start(2, q)
+
+    def sum_line(self, q, rows, buffer):
+        z, y = self.where[:2]
+        value = self.g[(q % 8, z, y) + rows].astype(jnp.float32)
+        for d in range(3):
+            value += buffer[self.slot[q], d].astype(jnp.float32)
+        self.g[(q % 8, z, y) + rows] = value.astype(jnp.bfloat16)
+
+    def three(self, q):
+        y, at = self.where[1], self.slot[q]
+        self.arrive(2, q)
+        if self.crosswise[q]:
+
+            @pl.loop(0, 4)
+            def _(zi):
+                add_into(self.g, (q % 8, zi, y, self.near), self.ya, (at, zi))
+
+        else:
+            self.sum_line(q, (), self.zb)
+        self.start(3, q)
+
+    def export(self, q):
+        target = self.totals[0].at[q] if q < 8 else self.totals[1].at[q - 8]
+        return pltpu.make_async_copy(self.stage.at[q % 4], target, self.out_sem.at[q])
+
+    def four(self, q):
+        z, y = self.where[:2]
+        at = self.slot[q]
+        self.arrive(3, q)
+        if self.crosswise[q]:
+            self.sum_line(q, (self.near,), self.za)
+            self.start(4, q)
+        else:
+            if q >= 4:
+                self.export(q - 4).wait()
+            self.stage[q % 4] = self.g[q % 8, z, y].astype(jnp.float32) + self.xb[at].astype(jnp.float32)
+            self.export(q).start()
+
+    def five(self, q):
+        z, y = self.where[:2]
+        if self.crosswise[q]:
+            self.arrive(4, q)
+            if q >= 4:
+                self.export(q - 4).wait()
+            self.stage[q % 4, self.near] = self.g[q % 8, z, y, self.near].astype(jnp.float32)
+            self.stage[q % 4, self.far] = self.fa[self.slot[q]].astype(jnp.float32)
+            self.export(q).start()
+
+    def run(self, calls):
+        for name, q in calls:
+            getattr(self, name)(q)
+
+    def finish(self):
+        count = len(self.crosswise)
+        for q in range(count - 4, count):
+            self.export(q).wait()
+        for stage in range(5):
+            for q in range(count):
+                if (stage, q) not in self.waited:
+                    self.sent(q, (stage,))
+
+    @staticmethod
+    def scratch(crosswise):
+        dma, vmem, low = pltpu.SemaphoreType.DMA, pltpu.VMEM, jnp.bfloat16
+        n, across = len(crosswise), sum(crosswise)
+        along = n - across
+        return [
+            vmem((12, 4, 2, 128, WIDE), low),
+            vmem((4, 4, 2, 128, WIDE), low),
+            vmem((across, 4, 2, 64, WIDE), low),
+            vmem((across, 4, 64, WIDE), low),
+            vmem((across, 3, 64, WIDE), low),
+            vmem((across, 64, WIDE), low),
+            vmem((along, 4, 128, WIDE), low),
+            vmem((along, 3, 128, WIDE), low),
+            vmem((along, 128, WIDE), low),
+            vmem((4, 128, WIDE), jnp.float32),
+            dma((n,)), dma((n,)), dma((n,)), dma((n,)), dma((n, 3)), dma((n, 3)),
+            dma((n, 3)), dma((n, 3)), dma((n,)), dma((n,)), dma((n,)), pltpu.SemaphoreType.REGULAR((4,)),
+        ]
+
+
+class Spread:
+    def __init__(self, src, dst, sems):
+        z, y, x, c = place()
+        _, _, x_peer, c_peer = peers_of(z, y, x, c)
+        mine, theirs = 2 * x + c, 2 * (1 - x) + c
+        self.cross = remote(src.at[1 - x], dst.at[mine], sems.at[0], sems.at[1], x_peer)
+        self.near = remote(src.at[x], dst.at[mine], sems.at[2], sems.at[3], c_peer)
+        self.local = pltpu.make_async_copy(src.at[x], dst.at[mine], sems.at[4])
+        self.onward = remote(dst.at[theirs], dst.at[theirs], sems.at[5], sems.at[6], c_peer)
+
+    def start(self):
+        self.near.start()
+        self.local.start()
+
+    def forward(self):
+        self.cross.wait_recv()
+        self.onward.start()
+
+    def finish(self):
+        self.cross.wait_send()
+        self.near.wait()
+        self.local.wait()
+        self.onward.wait()
+
+
+def transpose_into(target, source):
+    for at in range(source.shape[1] // LANES):
+        target[pl.ds(at * LANES, LANES), :] = source[:, pl.ds(at * LANES, LANES)].T
+
+
+KINDS = (True, False) * 4 + (True, False, False, False)
+
+
+def both(name, tile):
+    return ((name, 2 * tile), (name, 2 * tile + 1))
+
+
+MLP_PLAN = {
+    0: both("begin", 0),
+    1: both("one", 0),
+    2: both("begin", 1),
+    3: both("one", 1) + both("two", 0),
+    4: both("begin", 2),
+    5: both("one", 2),
+    6: both("begin", 3) + both("two", 1) + both("three", 0),
+    7: both("one", 3) + both("four", 0),
+}
+OUTPUT_PLAN = both("five", 0) + both("two", 2)
+NORM_PLAN = both("three", 1)
+PAIR_PLAN = {
+    0: (("begin", 8),) + both("four", 1) + both("two", 3),
+    1: (("one", 8),) + both("three", 2) + both("five", 1),
+    2: (("begin", 9),) + both("four", 2) + both("three", 3),
+    3: (("one", 9), ("two", 8)) + both("five", 2),
+    4: (("begin", 10),) + both("four", 3),
+    5: (("one", 10), ("two", 9), ("three", 8)) + both("five", 3),
+    6: (("begin", 11), ("three", 9), ("four", 8)),
+    7: (("one", 11), ("two", 10), ("four", 9)),
+}
+DRAIN_PLAN = (("five", 8), ("three", 10), ("two", 11), ("four", 10), ("three", 11), ("four", 11))
+
+
+def back_body(
+    w, second_in, back_in, x_in, hidden_in, counts, qkv_in, heads_in, vectors,
+    total_m, total_q, out_spread, grad_spread, bias_grad, vec_out, qv_out,
+    tall, tall_t, back, back_t, halves, hidden, total_acc, grad_second, out_low, in_low, wv,
+    grad_part, parts, query_part, qkv_v, heads_v, vec_acc, *rest,
+):
+    ws, qs, hs, in_sems, out_sems, grad_sems = rest[:6]
+    z, y, x, c = place()
+    rs = Scatter(KINDS, rest[6:] + (total_m, total_q))
+    greet(rs.line + [rs.y_peer, rs.x_peer, rs.c_peer])
+    low, full = jnp.bfloat16, jnp.float32
+
+    def turn(s):
+        return (s % 2, s // 2) if isinstance(s, int) else (lax.rem(s, 2), lax.div(s, 2))
+
+    def side_of(s):
+        return lax.rem(1 - c + s, 2)
+
+    def tile_load(s):
+        slot, j = turn(s)
+        return pltpu.make_async_copy(w.at[pl.ds(4 + 2 * j, 2), side_of(s)], wv.at[slot], ws.at[slot])
+
+    def pair_loads(s):
+        slot, k = turn(s)
+        pair = side_of(s) * 4 + k
+        return [
+            pltpu.make_async_copy(w.at[k, side_of(s)], wv.at[slot, 0], ws.at[slot]),
+            pltpu.make_async_copy(qkv_in.at[pair], qkv_v.at[slot], qs.at[slot]),
+            pltpu.make_async_copy(
+                heads_in.at[:, columns(pair * LANES, LANES)], heads_v.at[slot], hs.at[slot]
+            ),
+        ]
+
+    def start(copies):
+        for copy in copies:
+            copy.start()
+
+    loads = [
+        pltpu.make_async_copy(src, dst, in_sems.at[at])
+        for at, (src, dst) in enumerate(
+            ((second_in, tall), (back_in, back), (hidden_in, hidden), (x_in, in_low))
+        )
+    ]
+    start(loads[:3])
+    tile_load(0).start()
+    tile_load(1).start()
+    loads[3].start()
+    grad_second[...] = jnp.zeros_like(grad_second)
+    loads[0].wait()
+    transpose_into(tall_t, tall)
+    loads[1].wait()
+    transpose_into(back_t, back)
+    loads[2].wait()
+    total_acc[...] = hidden[...] + vectors[7:8, :]
+
+    @pl.loop(0, 8)
+    def _(s):
+        slot, j = turn(s)
+        side = side_of(s)
+        tile_load(s).wait()
+        tile = side * 4 + j
+        bias = vectors[pl.ds(8 + side * 2 + lax.div(j, 2), 1), columns(lax.rem(j, 2) * WIDE, WIDE)]
+        up = wv[slot, 0].reshape(1024, WIDE)
+        down = wv[slot, 1].reshape(1024, WIDE)
+        sums = jnp.zeros((1, WIDE), full)
+        for half in range(2):
+            rows = pl.ds(half * SLOTS, SLOTS)
+            pre = nn(tall[rows, :], up) + bias
+            grad_active = nn(back[rows, :], down)
+            share = 0.5 * (1.0 + lax.erf(pre * 0.7071067811865476))
+            slope = share + pre * jnp.exp(-0.5 * pre * pre) * 0.3989422804014327
+            act = (pre * share).astype(low)
+            grad_pre = (grad_active * slope).astype(low)
+            halves[0, rows, :] = act
+            halves[1, rows, :] = grad_pre
+            sums += jnp.sum(grad_pre.astype(full), 0, keepdims=True)
+            total_acc[rows, :] += nt(act, down)
+            grad_second[rows, :] += nt(grad_pre, up)
+        bias_grad[pl.ds(tile, 1), :] = sums
+        for again in (4, 6):
+
+            @pl.when(s == again)
+            def _():
+                rs.sent(again - 4, (0,))
+                rs.sent(again - 3, (0,))
+
+        first = jnp.where(slot == 0, 8 + lax.rem(2 * j, 4), 2 * j)
+        for zi in range(4):
+            rows = pl.ds(zi * 256, 256)
+            rs.g[first, zi] = nn(tall_t[rows, :], halves[1]).astype(low).reshape(2, 128, WIDE)
+            rs.g[first + 1, zi] = nn(back_t[rows, :], halves[0]).astype(low).reshape(2, 128, WIDE)
+
+        @pl.when(s < 6)
+        def _():
+            tile_load(s + 2).start()
+
+        for done, calls in MLP_PLAN.items():
+
+            @pl.when(s == done)
+            def _():
+                rs.run(calls)
+
+    start(pair_loads(0))
+    start(pair_loads(1))
+    sent_out = Spread(out_low, out_spread, out_sems)
+    for first in (True, False):
+        half = 1 - x if first else x
+        out_low[half] = total_acc[aligned(half * SLOTS, SLOTS, SLOTS), :].astype(low)
+        if first:
+            sent_out.cross.start()
+    sent_out.start()
+    rs.run(OUTPUT_PLAN)
+    vec_acc[...] = jnp.zeros_like(vec_acc)
+
+    def fold(row, value):
+        vec_acc[row] += jnp.sum(value.reshape(-1, 8, value.shape[1]), 0)
+
+    step = 64
+    loads[3].wait()
+
+    @pl.loop(0, ROWS // step)
+    def _(at):
+        rows = pl.ds(pl.multiple_of(at * step, step), step)
+        half_rows = pl.ds(pl.multiple_of(lax.rem(at, 5) * step, step), step)
+        ones = vectors[5:6, :]
+        _, normal, inverse = norm_rows(hidden[rows, :], ones, vectors[6:7, :])
+        grad = grad_second[rows, :]
+        behind = back[rows, :].astype(full)
+        result = behind + norm_back(grad, normal, inverse, ones)
+        hidden[rows, :] = result
+        branch = result.astype(low)
+        back[rows, :] = branch
+        fold(2, branch.astype(full))
+        fold(3, grad * normal)
+        fold(4, grad)
+        fold(5, behind)
+        first, _, _ = norm_rows(
+            in_low[lax.div(at, 5), half_rows, :].astype(full), vectors[0:1, :], vectors[1:2, :]
+        )
+        tall[rows, :] = first.astype(low)
+
+    transpose_into(back_t, back)
+    transpose_into(tall_t, tall)
+    total_acc[...] = jnp.zeros_like(total_acc)
+    rs.run(NORM_PLAN)
+    sent_out.forward()
+    valid = slots_valid(counts, 0)
+    lane = lax.broadcasted_iota(jnp.int32, (1, LANES), 1)
+    line = lax.broadcasted_iota(jnp.int32, (LANES, 1), 0)
+
+    @pl.loop(0, 8)
+    def _(s):
+        slot, k = turn(s)
+        pair = side_of(s) * 4 + k
+        for copy in pair_loads(s):
+            copy.wait()
+        grad_heads = nn(back[...], wv[slot, 0, :, :, :, pl.ds(3 * LANES, LANES)].reshape(1024, LANES))
+        grad_heads = grad_heads.astype(low)
+        queries = qkv_v[slot, :, pl.ds(0, LANES)]
+        keys = qkv_v[slot, :, pl.ds(LANES, LANES)]
+        values = qkv_v[slot, :, pl.ds(2 * LANES, LANES)]
+        keys_t = keys.T
+        parts[...] = jnp.zeros_like(parts)
+        query_part[...] = jnp.zeros_like(query_part)
+
+        @pl.loop(0, 2)
+        def _(at):
+            here = (lane >= at * HD) & (lane < at * HD + HD)
+            own_keys = jnp.where(here, keys * jnp.bfloat16(0.125), jnp.zeros_like(keys))
+            own_values = jnp.where(here, values, jnp.zeros_like(values))
+            scores = jnp.where(valid, nt(own_keys, queries), -1000000000.0)
+            top = jnp.max(scores, 0, keepdims=True)
+            exponent = jnp.exp(scores - top)
+            attention = exponent * (1.0 / jnp.sum(exponent, 0, keepdims=True))
+            grad_attention = nt(own_values, grad_heads)
+            inner = jnp.sum(attention * grad_attention, 0, keepdims=True)
+            grad_scores = (attention * (grad_attention - inner)).astype(low)
+            own_line = (line >= at * HD) & (line < at * HD + HD)
+            query_part[...] += jnp.where(own_line, nn(keys_t, grad_scores), 0.0)
+            parts[0] += jnp.where(here, nn(grad_scores, queries), 0.0)
+            parts[1] += jnp.where(here, nn(attention.astype(low), grad_heads), 0.0)
+
+        grad_q = (query_part[...] * 0.125).T.astype(low)
+        grad_k = (parts[0] * 0.125).astype(low)
+        grad_v = parts[1].astype(low)
+        grad_part[:, pl.ds(0, LANES)] = grad_q
+        grad_part[:, pl.ds(LANES, LANES)] = grad_k
+        grad_part[:, pl.ds(2 * LANES, LANES)] = grad_v
+        qv_out[pl.ds(pair, 1), :] = jnp.sum(grad_q.astype(full), 0, keepdims=True)
+        qv_out[pl.ds(8 + pair, 1), :] = jnp.sum(grad_v.astype(full), 0, keepdims=True)
+        for half in range(2):
+            rows = pl.ds(half * SLOTS, SLOTS)
+            total_acc[rows, :] += nt(
+                grad_part[rows, :], wv[slot, 0, :, :, :, pl.ds(0, 3 * LANES)].reshape(1024, 3 * LANES)
+            )
+        for again in range(4):
+
+            @pl.when(s == 2 * again)
+            def _():
+                rs.sent(4 + again, (0,))
+
+            @pl.when(s == 2 * again + 1)
+            def _():
+                rs.sent(again, (1, 2, 3, 4))
+
+        target = jnp.where(slot == 0, 8 + k, k)
+        for zi in range(4):
+            rows = pl.ds(zi * 256, 256)
+            rs.g[target, zi, :, :, pl.ds(0, 3 * LANES)] = (
+                nn(tall_t[rows, :], grad_part[...]).astype(low).reshape(2, 128, 3 * LANES)
+            )
+            rs.g[target, zi, :, :, pl.ds(3 * LANES, LANES)] = (
+                nn(back_t[rows, :], heads_v[slot]).astype(low).reshape(2, 128, LANES)
+            )
+
+        @pl.when(s < 6)
+        def _():
+            start(pair_loads(s + 2))
+
+        for done, calls in PAIR_PLAN.items():
+
+            @pl.when(s == done)
+            def _():
+                rs.run(calls)
+
+    sent_grad = Spread(in_low, grad_spread, grad_sems)
+    for first in (True, False):
+        half = 1 - x if first else x
+
+        @pl.loop(0, SLOTS // step)
+        def _(at):
+            half_rows = pl.ds(pl.multiple_of(at * step, step), step)
+            rows = aligned(half * SLOTS + at * step, step, step)
+            ones = vectors[0:1, :]
+            _, normal, inverse = norm_rows(in_low[half, half_rows, :].astype(full), ones, vectors[1:2, :])
+            grad = total_acc[rows, :]
+            fold(0, grad * normal)
+            fold(1, grad)
+            result = hidden[rows, :] + norm_back(grad, normal, inverse, ones)
+            in_low[half, half_rows, :] = result.astype(low)
+
+        if first:
+            sent_grad.cross.start()
+    sent_grad.start()
+    for row in range(6):
+        vec_out[pl.ds(row, 1), :] = jnp.sum(vec_acc[row], 0, keepdims=True)
+    rs.run(DRAIN_PLAN)
+    sent_grad.forward()
+    sent_out.finish()
+    sent_grad.finish()
+    rs.finish()
+
+
+def back_all(w, second, back, x_all, hidden, counts, qkv, heads, vectors):
+    dma, vmem = pltpu.SemaphoreType.DMA, pltpu.VMEM
+    low, full = jnp.bfloat16, jnp.float32
+    anywhere = pl.BlockSpec(memory_space=pl.ANY)
+    in_vmem = pl.BlockSpec(memory_space=pltpu.VMEM)
+    shape = jax.ShapeDtypeStruct
+    width = second.shape[1]
+    return pl.pallas_call(
+        back_body,
+        out_shape=(
+            shape((8, 128, WIDE), full),
+            shape((4, 128, WIDE), full),
+            shape((4, SLOTS, width), low),
+            shape((4, SLOTS, width), low),
+            shape((8, WIDE), full),
+            shape((8, width), full),
+            shape((16, LANES), full),
+        ),
+        in_specs=[anywhere] * 5 + [in_vmem] + [anywhere] * 2 + [in_vmem],
+        out_specs=(anywhere,) * 4 + (in_vmem,) * 3,
+        scratch_shapes=[
+            vmem((ROWS, width), low),
+            vmem((width, ROWS), low),
+            vmem((ROWS, width), low),
+            vmem((width, ROWS), low),
+            vmem((2, ROWS, WIDE), low),
+            vmem((ROWS, width), full),
+            vmem((ROWS, width), full),
+            vmem((ROWS, width), full),
+            vmem((2, SLOTS, width), low),
+            vmem((2, SLOTS, width), low),
+            vmem((2, 2, 4, 2, 128, WIDE), low),
+            vmem((ROWS, 3 * LANES), low),
+            vmem((2, ROWS, LANES), full),
+            vmem((LANES, ROWS), full),
+            vmem((2, ROWS, 3 * LANES), low),
+            vmem((2, ROWS, LANES), low),
+            vmem((6, 8, width), full),
+            dma((2,)), dma((2,)), dma((2,)), dma((4,)), dma((7,)), dma((7,)),
+        ] + Scatter.scratch(KINDS),
+        compiler_params=pltpu.CompilerParams(
+            collective_id=1, has_side_effects=True, vmem_limit_bytes=62 * MIB
+        ),
+    )(w, second, back, x_all, hidden, counts, qkv, heads, vectors)
+
+
+TILES = (
+    [t for t in range(16) if t % 4 < 3],
+    [3, 7, 11, 15],
+    [t for t in range(16, 48) if t // 4 % 2 == 0],
+    [t for t in range(16, 48) if t // 4 % 2 == 1],
+)
+SIZES = (3072.0 * 1024.0, 1024.0 * 1024.0, 4096.0 * 1024.0, 4096.0 * 1024.0)
+VECS = 12
+MISC = 12
+SUMS = 14
+
+
+def col_of(refs, t):
+    chunk, part = t // 4, t % 4
+    if chunk < 4:
+        if part < 3:
+            return refs[0].at[pl.ds(part, 1), pl.ds(chunk * LANES, LANES)]
+        return refs[1].at[pl.ds(chunk, 1), :]
+    return refs[2 + chunk % 2].at[pl.ds((chunk - 4) // 2 * 4 + part, 1), :]
+
+
+def factor_body(
+    total_q, total_m, squares, vec_sums, qv_sums, bias_grad, vecs, moments,
+    row_mix, col_out, row_up, col_down, col_mix, row_out, col_up, row_down,
+    row_new, row_flat, new_mix, new_out, new_up, new_down, vec_grad, vec_moment, vec_new, scale,
+    core_s, core_r, pack_s, pack_r, ctx_r, line_s, line_r, y_r, last_s, last_r,
+    c_ss, c_rs, x_ss, x_rs, z_ss, z_rs, y_ss, y_rs, l_ss, l_rs,
+):
+    z, y, x, c = place()
+    line, y_peer, x_peer, c_peer = peers_of(z, y, x, c)
+    square_peers = []
+    for step in range(1, 16):
+        spot = lax.rem((z * 2 + y) * 2 + c + step, 16)
+        square_peers.append((lax.div(spot, 2), x, lax.rem(spot, 2)))
+    greet(square_peers + [x_peer])
+
+    def tile_of(t):
+        cols = pl.ds(t % 4 * LANES, LANES)
+        return total_q[t // 4, :, cols] if t < 16 else total_m[t // 4 - 4, :, cols]
+
+    def lanes(at):
+        return pl.ds(at % 8 * LANES, LANES)
+
+    lane = lax.broadcasted_iota(jnp.int32, (128, 128), 1)
+    core_s[pl.ds(0, 2), :] = vec_sums[pl.ds(0, 2), :]
+    for at in range(8):
+        core_s[pl.ds(2, 1), lanes(at)] = qv_sums[pl.ds(at, 1), :]
+        core_s[pl.ds(3, 1), lanes(at)] = qv_sums[pl.ds(8 + at, 1), :]
+        core_s[pl.ds(8 + at // 2, 1), pl.ds(at % 2 * WIDE, WIDE)] = bias_grad[pl.ds(at, 1), :]
+    core_s[pl.ds(4, 4), :] = vec_sums[pl.ds(2, 4), :]
+    packed = jnp.zeros((128, 128), jnp.float32)
+    sums, olds = [], []
+    old_cols = (col_mix, row_out, col_up, row_down)
+    for m in range(4):
+        block = jnp.zeros((128, 128), jnp.float32)
+        old = jnp.zeros((1, LANES), jnp.float32)
+        for t in TILES[m]:
+            tile = tile_of(t)
+            tile = tile * tile
+            line_s[pl.ds(SUMS + t // 8, 1), lanes(t)] = jnp.sum(tile, 0, keepdims=True)
+            block += tile
+            old += col_of(old_cols, t)[...]
+        per_row = jnp.sum(block, 1, keepdims=True)
+        packed = jnp.where((lane >= 32 * m) & (lane < 32 * m + 32), per_row, packed)
+        sums.append(jnp.sum(per_row, 0, keepdims=True))
+        if m % 2 == 0:
+            olds.append(jnp.sum((row_mix, None, row_up)[m][...], 1, keepdims=True) * 0.5)
+        else:
+            olds.append(jnp.sum(old, 1, keepdims=True) * 0.125)
+    pack_s[...] = packed
+    misc = sums + [squares[pl.ds(m, 1), 0:1] for m in range(4)] + olds + [jnp.zeros((1, 1), jnp.float32)] * 4
+    for at, value in enumerate(misc):
+        core_s[pl.ds(MISC + at // 8, 1), lanes(at)] = jnp.broadcast_to(value, (1, LANES))
+    core_s[pl.ds(14, 2), :] = jnp.zeros((2, 1024), jnp.float32)
+    hops = [
+        remote(core_s, core_r, c_ss.at[0], c_rs.at[0], c_peer),
+        remote(pack_s, pack_r, c_ss.at[1], c_rs.at[1], c_peer),
+    ]
+    for hop in hops:
+        hop.start()
+    for hop in hops:
+        hop.wait()
+    core_r[...] = core_r[...] + core_s[...]
+    hop = remote(core_r, ctx_r, x_ss.at[0], x_rs.at[0], x_peer)
+    hop.start()
+    hop.wait()
+    line_s[pl.ds(0, VECS), :] = core_r[pl.ds(0, VECS), :] + ctx_r[pl.ds(0, VECS), :]
+    line_s[pl.ds(VECS, 2), :] = core_r[pl.ds(VECS, 2), :]
+    line_s[pl.ds(20, 4), :] = jnp.zeros((4, 1024), jnp.float32)
+    hops = [
+        remote(line_s, line_r.at[z], z_ss.at[at], z_rs.at[at], peer) for at, peer in enumerate(line)
+    ]
+    for hop in hops:
+        hop.start()
+    line_r[pl.ds(z, 1)] = line_s[...][None]
+    for hop in hops:
+        hop.wait()
+    line_s[...] = (line_r[0] + line_r[1]) + (line_r[2] + line_r[3])
+    hop = remote(line_s, y_r, y_ss.at[0], y_rs.at[0], y_peer)
+    hop.start()
+    hop.wait()
+    line_s[...] = line_s[...] + y_r[...]
+    grads = line_s[pl.ds(0, VECS), :]
+    vec_grad[...] = grads
+    moment = decay_rate * moments[...] + (1.0 - decay_rate) * grads * grads
+    vec_moment[...] = moment
+    vec_step = grads * lax.rsqrt(moment)
+    new_cols = (new_mix, new_out, new_up, new_down)
+    for t in range(48):
+        col_of(new_cols, t)[...] = decay_rate * col_of(old_cols, t)[...] + (1.0 - decay_rate) * (
+            line_s[pl.ds(SUMS + t // 8, 1), lanes(t)] * (1.0 / 1024.0)
+        )
+    row_sum = pack_r[...] + pack_s[...]
+    row_count = jnp.where(lane < 32, 1.0 / 3072.0, jnp.where(lane < 64, 1.0 / 1024.0, 1.0 / 4096.0))
+    row_old = jnp.concatenate(
+        [jnp.broadcast_to(one[...], (32, LANES)) for one in (row_mix, col_out, row_up, col_down)], 0
+    ).T
+    row_all = decay_rate * row_old + (1.0 - decay_rate) * row_sum * row_count
+    row_new[...] = row_all
+    row_flat[...] = row_all.T
+    row_inverse = lax.rsqrt(row_all)
+    row_lengths = (1024.0, 1024.0, 1024.0, 4096.0)
+    square = jnp.zeros((1, 1), jnp.float32)
+    factors = []
+    for m in range(4):
+        all_square, all_weight, all_old = (
+            line_s[pl.ds(MISC + at // 8, 1), pl.ds(at % 8 * LANES, 1)] for at in (m, 4 + m, 8 + m)
+        )
+        average = decay_rate * all_old / row_lengths[m] + (1.0 - decay_rate) * all_square / SIZES[m]
+        block = jnp.zeros((128, 128), jnp.float32)
+        for t in TILES[m]:
+            update = tile_of(t) * lax.rsqrt(col_of(new_cols, t)[...])
+            block += update * update
+        by_row = row_inverse[:, 32 * m : 32 * m + 1]
+        per_row = jnp.sum(block, 1, keepdims=True) * by_row * by_row
+        square += jnp.sum(per_row, 0, keepdims=True) * average
+        factors.append((jnp.sqrt(average), jnp.sqrt(all_weight / SIZES[m])))
+    spot = (z * 2 + y) * 2 + c
+    last_s[...] = jnp.broadcast_to(square, (8, LANES))
+    last_r[pl.ds(spot, 1)] = last_s[...][None]
+    hops = [
+        remote(last_s, last_r.at[spot], l_ss.at[at], l_rs.at[at], peer)
+        for at, peer in enumerate(square_peers)
+    ]
+    for hop in hops:
+        hop.start()
+    for hop in hops:
+        hop.wait()
+    square = jnp.zeros((1, 1), jnp.float32)
+    for at in range(16):
+        square += last_r[at, 0:1, 0:1]
+    vec_square = jnp.sum(jnp.sum(vec_step * vec_step, 1, keepdims=True), 0, keepdims=True)
+    old_vecs = vecs[...]
+    vec_size = VECS * 1024.0
+    vec_mean = jnp.sum(jnp.sum(old_vecs * old_vecs, 1, keepdims=True), 0, keepdims=True) / vec_size
+    count = sum(SIZES) + vec_size
+    shrink = 1.0 / jnp.maximum(1.0, jnp.sqrt((square + vec_square) / count) / clip_level)
+    vec_new[...] = old_vecs - step_rate * jnp.sqrt(vec_mean) * vec_step * shrink
+    for m in range(4):
+        scale[pl.ds(m, 1), :] = jnp.broadcast_to(
+            step_rate * factors[m][0] * factors[m][1] * shrink, (1, LANES)
+        )
+    scale[pl.ds(4, 4), :] = jnp.zeros((4, LANES), jnp.float32)
+
+
+def factor_all(*arrays):
+    dma = pltpu.SemaphoreType.DMA
+    full = jnp.float32
+    in_vmem = pl.BlockSpec(memory_space=pltpu.VMEM)
+    shape = jax.ShapeDtypeStruct
+    shapes = [(128, 128), (128, 128), (3, WIDE), (4, LANES), (16, LANES), (16, LANES)]
+    shapes += [(VECS, 1024)] * 3 + [(8, LANES)]
+    return pl.pallas_call(
+        factor_body,
+        out_shape=tuple(shape(one, full) for one in shapes),
+        in_specs=[in_vmem] * len(arrays),
+        out_specs=(in_vmem,) * len(shapes),
+        scratch_shapes=[
+            pltpu.VMEM((16, 1024), full),
+            pltpu.VMEM((16, 1024), full),
+            pltpu.VMEM((128, 128), full),
+            pltpu.VMEM((128, 128), full),
+            pltpu.VMEM((16, 1024), full),
+            pltpu.VMEM((24, 1024), full),
+            pltpu.VMEM((4, 24, 1024), full),
+            pltpu.VMEM((24, 1024), full),
+            pltpu.VMEM((8, LANES), full),
+            pltpu.VMEM((16, 8, LANES), full),
+            dma((2,)), dma((2,)), dma((1,)), dma((1,)), dma((3,)), dma((3,)), dma((1,)), dma((1,)),
+            dma((15,)), dma((15,)),
+        ],
+        compiler_params=pltpu.CompilerParams(
+            collective_id=3, has_side_effects=True, vmem_limit_bytes=40 * MIB
+        ),
+    )(*arrays)
+
+
+def finish_body(
+    total_q, total_m, mix_w, out_w, up_w, down_w, row_new, row_flat, new_mix, new_out, new_up, new_down,
+    vec_grad, vec_moment, vec_new, scale, *outs,
+):
+    grads, news, copies, smalls = outs[:4], outs[4:8], outs[8:12], outs[12:]
+    at = pl.program_id(0)
+
+    def by_row(m):
+        return lax.rsqrt(row_new[:, 32 * m : 32 * m + 1])
+
+    def by_col(row, m):
+        return lax.rsqrt(row) * scale[pl.ds(m, 1), :]
+
+    def put(m, index, grad, old, update):
+        new = old - grad * update
+        grads[m][index] = grad
+        news[m][index] = new
+        copies[m][index] = new.astype(jnp.bfloat16)
+
+    everything = slice(None)
+    for part in range(3):
+        cols = new_mix[pl.ds(part, 1), columns(at * LANES, LANES)]
+        grad = total_q[0, :, pl.ds(part * LANES, LANES)]
+        put(0, (part, everything, everything), grad, mix_w[part], by_row(0) * by_col(cols, 0))
+    turned_out = lax.rsqrt(row_flat[pl.ds(32, 1), :])
+    turned_down = lax.rsqrt(row_flat[pl.ds(96, 1), :])
+    cols = jnp.broadcast_to(by_col(new_out[pl.ds(at, 1), :], 1), (LANES, LANES)).T
+    grad = total_q[0, :, pl.ds(3 * LANES, LANES)].T
+    put(1, (everything, everything), grad, out_w[...], cols * turned_out)
+    for part in range(4):
+        here = pl.ds(part * LANES, LANES)
+        row = pl.ds(at * 4 + part, 1)
+        put(
+            2, (everything, here), total_m[0, :, here], up_w[:, here],
+            by_row(2) * by_col(new_up[row, :], 2),
+        )
+        cols = jnp.broadcast_to(by_col(new_down[row, :], 3), (LANES, LANES)).T
+        put(3, (here, everything), total_m[1, :, here].T, down_w[here, :], cols * turned_down)
+    for target, source in zip(smalls[:7], (vec_grad, vec_moment, vec_new, new_mix, new_out, new_up, new_down)):
+        target[...] = source[...]
+    for m, target in enumerate(smalls[7:]):
+        target[...] = row_flat[pl.ds(32 * m, 1), :]
+
+
+def finish_all(total_q, total_m, weights, factors):
+    low, full = jnp.bfloat16, jnp.float32
+    shape = jax.ShapeDtypeStruct
+    blocks = [
+        pl.BlockSpec((3, 128, LANES), lambda at: (0, 0, at)),
+        pl.BlockSpec((LANES, 128), lambda at: (at, 0)),
+        pl.BlockSpec((128, WIDE), lambda at: (0, at)),
+        pl.BlockSpec((WIDE, 128), lambda at: (at, 0)),
+    ]
+
+    def whole(array_shape):
+        return pl.BlockSpec(array_shape, lambda at: (0,) * len(array_shape))
+
+    smalls = [(VECS, 1024)] * 3 + [(3, WIDE), (4, LANES), (16, LANES), (16, LANES)] + [(1, LANES)] * 4
+    shapes = [shape(one.shape, kind) for kind in (full, full, low) for one in weights]
+    shapes += [shape(one, full) for one in smalls]
+    return pl.pallas_call(
+        finish_body,
+        grid=(4,),
+        out_shape=tuple(shapes),
+        in_specs=[
+            pl.BlockSpec((1, 128, WIDE), lambda at: (at, 0, 0)),
+            pl.BlockSpec((2, 128, WIDE), lambda at: (at, 0, 0)),
+        ] + blocks + [whole(one.shape) for one in factors],
+        out_specs=tuple(blocks * 3 + [whole(one) for one in smalls]),
+        compiler_params=pltpu.CompilerParams(vmem_limit_bytes=40 * MIB),
+    )(total_q, total_m, *weights, *factors)
+
+
+def fast_body(
+    inputs, cotangent, key_mask, image_mask, qkv_weight, out_weight, up_weight, down_weight,
+    vectors, row_qkv, col_qkv, row_out, col_out, row_up, col_up, row_down, col_down, vector_moments,
+):
+    images, tokens, width = inputs.shape
+    pad = ((0, 0), (0, SLOTS - tokens), (0, 0))
+    weight_rows = (key_mask * image_mask[:, None]).astype(jnp.bfloat16)
+    x_in = jnp.pad(inputs, pad)
+    b_in = jnp.pad(cotangent * weight_rows[:, :, None], pad)
+    counts = jnp.sum(key_mask, 1).astype(jnp.float32)
+    n_in = jnp.broadcast_to(counts[:, None, None], (images, 8, LANES))
+    weights = (qkv_weight.transpose(1, 0, 2), out_weight, up_weight, down_weight)
+    w, b_all, x_all, n_all, qkv, heads, hidden, second, squares = front_all(
+        x_in, b_in, n_in, weights, vectors
+    )
+    total_m, total_q, out_spread, grad_spread, bias_grad, vec_sums, qv_sums = back_all(
+        w, second, b_all.reshape(ROWS, width), x_all, hidden, n_all, qkv, heads, vectors
+    )
+    factors = factor_all(
+        total_q, total_m, squares, vec_sums, qv_sums, bias_grad, vectors, vector_moments,
+        row_qkv.reshape(1, LANES), col_out.reshape(1, LANES), row_up.reshape(1, LANES),
+        col_down.reshape(1, LANES), col_qkv, row_out.reshape(4, LANES), col_up.reshape(16, LANES),
+        row_down.reshape(16, LANES),
+    )
+    done = finish_all(total_q, total_m, weights, factors)
+
+    def natural(four):
+        return (four[0].transpose(1, 0, 2),) + tuple(four[1:])
+
+    vector_grad, vector_moment, vector_new, new_mix, new_out, new_up, new_down = done[12:19]
+    rows = [one.reshape(-1) for one in done[19:]]
+    return (
+        (out_spread[:, :tokens], grad_spread[:, :tokens])
+        + natural(done[:4])
+        + (vector_grad,)
+        + natural(done[4:8])
+        + (vector_new,)
+        + natural(done[8:12])
+        + (
+            rows[0], new_mix, new_out.reshape(-1), rows[1], rows[2], new_up.reshape(-1),
+            new_down.reshape(-1), rows[3], vector_moment,
+        )
+    )
+
+
+def pick_body(*arrays):
+    sizes = tuple(lax.axis_size(name) for name in ("fsdp", "ctx", "tp"))
+    if sizes == (8, 2, 2) and arrays[0].shape == (4, 290, 1024) and arrays[6].shape == (128, 2048):
+        return fast_body(*arrays)
+    return body(*arrays)
+
+
 def solution(mesh):
     placed = (
         P("fsdp", "ctx", None),
@@ -457,7 +1629,7 @@
         P(),
     )
     return jax.shard_map(
-        body,
+        pick_body,
         mesh=mesh,
         in_specs=placed,
         out_specs=(

time: 1440 us -> 388 us (0.27)
  waiting for transfers between devices: 959 us -> 0 us
  Pallas kernels: 0 us -> 365 us
  matrix products: 153 us -> 0 us
  other arithmetic: 122 us -> 3.94 us
  local copies, waits for them, and re-layouts: 130 us -> 14.5 us
  blocking collectives: 39 us -> 0 us
  between operations: 31.1 us -> 1.29 us
    reduce_scatter x4 -> x0, waiting for transfers between devices: 427 us -> none  [the longest x1 150 us: body(): lax.psum_scatter(grad_up, 'fsdp', scatter_dimension=0, tiled=True)]
    pallas_call x0 -> x4, Pallas kernels: none -> 365 us  [the longest x1 191 us: back_all(): pl.pallas_call(back_body, out_shape=(shape((8, 128, WIDE), full), shape((...]
    all_gather x6 -> x0, waiting for transfers between devices: 233 us -> none  [the longest x1 69.1 us: body(): lax.all_gather(up_weight.astype(jnp.bfloat16), 'fsdp', axis=0, tiled=True)]
    psum x5 -> x0, waiting for transfers between devices: 203 us -> none  [the longest x1 110 us: body(): lax.psum((vector_part, place_at(jnp.sum(mix_square, (1, 2)), (model_width...]
    dot_general x26 -> x0, matrix products: 153 us -> none  [the longest x2 14 us: attend_back(): jnp.einsum('gqhe,gkhe->ghqk', grad_heads, value_rows, preferred_element_t...]
    unnamed x17 -> x0, waiting for transfers between devices: 96.3 us -> none
    reduce_sum x33 -> x1, other arithmetic: 70.6 us -> 0.88 us  [fast_body(): counts = jnp.sum(key_mask, 1).astype(jnp.float32)]
    convert_element_type x15 -> x1, other arithmetic: 41.8 us -> 0.01 us  [fast_body(): counts = jnp.sum(key_mask, 1).astype(jnp.float32)]
  transfers between devices with their start and end apart: 16 -> 0, of which waited for: 15 -> 0; matrix products, arithmetic and copies ran while one was open for 16% -> 0% of each run, Pallas kernels for 0% -> 0%
where the time goes in v1:
time: 388 us; the launch traced here: 385 us
  Pallas kernels  365 us (94%)
  local copies, waits for them, and re-layouts  14.5 us (4%)
  other arithmetic  3.94 us (1%)
    pallas_call x1, Pallas kernels, back_all(): pl.pallas_call(back_body, out_shape=(shape((8, 128, WIDE), full), shape((...  191 us
    pallas_call x1, Pallas kernels, front_all(): pl.pallas_call(front_body, out_shape=(shape((CHUNKS, 2, 4, 2, 128, WIDE),...  140 us
    pallas_call x1, Pallas kernels, factor_all(): pl.pallas_call(factor_body, out_shape=tuple((shape(one, full) for one in...  30.8 us
    unnamed x47, local copies, waits for them, and re-layouts  8.15 us

profile of v1, /device:TPU:0, one launch (start us, length us, event | category | flops | bytes accessed | tf_op | source)
XLA Modules:
  0.0 384.7 jit_solution(5067823232131619655)
XLA Ops:
  0.7 0.9 fusion
  1.6 0.7 broadcast_in_dim.2.n_in
  2.2 3.1 copy_multiply_fusion
  5.3 0.0 copy-start.20
  5.3 1.8 pad.8.b_in
  7.1 0.8 copy-done.20
  7.9 0.7 copy.43
  8.7 1.7 pad.7.x_in
  10.4 139.6 %shard_map.369 = (bf16[12,2,4,2,128,512]{5,4,3,2,1,0:T(8,128)(2,1)}, bf16[2,320,1024]{2,1,0:T(8,128)(2,1)}, bf16[2,320,1024]{2,1,0:T(8,128)(2,1)}, f32[2,8,128]{...) custom-call(bf16[4,320,1024]{2,1,0:T(8,128)(2,1)} %pad.7.x_in, ...), custom_call_target="tpu_custom_call" | custom-call | tf_op jit(solution)/shard_map/pallas_call | solution.py:707
  150.0 190.5 %shard_map.370 = (f32[8,128,512]{2,1,0:T(8,128)}, f32[4,128,512]{2,1,0:T(8,128)}, bf16[4,320,1024]{2,1,0:T(8,128)(2,1)}, bf16[4,320,1024]{2,1,0:T(8,128)(2,1)}, ...) custom-call(bf16[12,2,4,2,128,512]{5,4,3,2,1,0:T(8,128)(2,1)} %get-tuple-element.74.w, ...), custom_call_target="tpu_custom_call" | custom-call | tf_op jit(solution)/shard_map/pallas_call | solution.py:1249
  340.5 1.9 slice.6
  342.5 0.0 copy-start.7
  342.5 0.0 copy-start.10
  342.6 0.0 copy-start.15
  342.6 0.0 copy-start.16
  342.6 0.0 copy-start.19
  342.6 3.2 copy.45
  346.0 30.8 %shard_map.371 = (f32[128,128]{1,0:T(8,128)S(1)}, f32[128,128]{1,0:T(8,128)S(1)}, f32[3,512]{1,0:T(4,128)S(1)}, f32[4,128]{1,0:T(4,128)S(1)}, f32[16,128]{1,0:T(...) custom-call(f32[4,128,512]{2,1,0:T(8,128)S(1)} %copy-done.1, ...), custom_call_target="tpu_custom_call" | custom-call | tf_op jit(solution)/shard_map/pallas_call | solution.py:1460
  376.8 0.2 slice.7
  377.1 0.0 copy-start.2
  377.1 0.0 copy-start.3
  377.1 0.0 copy-start.5
  377.1 3.2 copy.46
  380.4 4.0 %shard_map.372 = (f32[3,128,512]{2,1,0:T(8,128)}, f32[512,128]{1,0:T(8,128)}, f32[128,2048]{1,0:T(8,128)}, f32[2048,128]{1,0:T(8,128)}, f32[3,128,512]{2,1,0:T(8...) custom-call(f32[4,128,512]{2,1,0:T(8,128)S(1)} %copy-done.1, ...), custom_call_target="tpu_custom_call" | custom-call | tf_op jit(solution)/shard_map/pallas_call | solution.py:1545
  (35 shorter events, 0.1 us)
Async XLA Ops:
  5.3 2.6 copy-start.20
  342.4 3.4 copy-start
  342.4 3.4 copy-start.1
  342.5 3.4 copy-start.6
  342.5 3.4 copy-start.7
  342.5 3.4 copy-start.8
  342.5 3.4 copy-start.9
  342.5 3.4 copy-start.10
  342.5 3.4 copy-start.11
  342.5 3.4 copy-start.12
  342.5 3.4 copy-start.13
  342.6 3.4 copy-start.14
  342.6 3.4 copy-start.15
  342.6 3.4 copy-start.16
  342.6 3.4 copy-start.17
  342.6 3.4 copy-start.18
  342.6 3.4 copy-start.19
  346.0 30.8 %copy-start.21 = (bf16[4,320,1024]{2,1,0:T(8,128)(2,1)S(1)}, bf16[4,320,1024]{2,1,0:T(8,128)(2,1)}, u32[]{:S(2)}) copy-start(bf16[4,320,1024]{2,1,0:T(8,128)(2,1)} %get-tuple-element.83) | copy-start | bytes 7864324
  377.1 3.3 copy-start.2
  377.1 3.3 copy-start.3
  377.1 3.3 copy-start.4
  377.1 3.3 copy-start.5

commit v2 on v1

--- a/solution.py
+++ b/solution.py
@@ -508,11 +508,24 @@
     return jnp.sum(total, 1, keepdims=True)
 
 
+def arrival_time(event):
+    kind, k = event
+    return k + kind * (1.1 if k < 2 else 2.1)
+
+
+ARRIVALS = sorted(((kind, k) for k in range(CHUNKS) for kind in range(4)), key=arrival_time)
+
+
+def transpose_into(target, source):
+    for at in range(source.shape[1] // LANES):
+        target[pl.ds(at * LANES, LANES), :] = source[:, pl.ds(at * LANES, LANES)].T
+
+
 def front_body(
     x_in, b_in, n_in, mix_w, out_w, up_w, down_w, vectors,
-    kept, b_out, x_out, n_out, qkv, heads, hidden, second, squares,
-    normed, w, wo,
-    local, in_s, in_r, zs, zr, ys, yr, xs, xr, cs, cr, ws,
+    kept, g_out, b_out, x_out, n_out, qkv, heads, hidden, squares, grad_second, image_out, bias_grad,
+    normed, w, wo, normed_t, back_t, halves, total_acc, staged,
+    local, in_s, in_r, zs, zr, ys, yr, xs, xr, cs, cr, ws, gs,
 ):
     z, y, x, c = place()
     line, y_peer, x_peer, c_peer = peers_of(z, y, x, c)
@@ -540,7 +553,7 @@
     ]
 
     def share(odd):
-        size = 80 if odd else 96
+        size = 96
         return aligned(x * (128 - size), size, 16), aligned(x * size, 128 - size, 16)
 
     def z_copies(k, odd):
@@ -574,37 +587,38 @@
 
     ahead = 2
 
-    def within(k):
-        return not isinstance(k, int) or 0 <= k < CHUNKS
-
-    def link_step(t, odd):
-        if within(t):
-            arrive(z_copies(t, odd))
-            start(y_copies(t, odd))
-        if isinstance(t, int):
-            if within(t + ahead):
-                start(z_copies(t + ahead, odd))
+    def serve(kind, k):
+        odd = k % 2 == 1
+        if kind == 0:
+            arrive(z_copies(k, odd))
+            start(y_copies(k, odd))
+            if k + ahead < CHUNKS:
+                start(z_copies(k + ahead, odd))
+        elif kind == 1:
+            arrive(y_copies(k, odd))
+            start(x_copies(k, odd))
+        elif kind == 2:
+            arrive(x_copies(k, odd))
+            start(c_copies(k))
         else:
-
-            @pl.when(t + ahead < CHUNKS)
-            def _():
-                start(z_copies(t + ahead, odd))
-
-        if within(t - 2):
-            arrive(y_copies(t - 2, odd))
-            start(x_copies(t - 2, odd))
-        if within(t - 4):
-            arrive(x_copies(t - 4, odd))
-            start(c_copies(t - 4))
-        if within(t - 6):
-            arrive(c_copies(t - 6))
-            keep(t - 6).start()
+            arrive(c_copies(k))
+            if k < 4:
+                keep(k).start()
+
+    events = list(ARRIVALS)
+
+    def serve_some(count):
+        for _ in range(min(count, len(events))):
+            serve(*events.pop(0))
+
+    def serve_until(k):
+        while (3, k) in events:
+            serve(*events.pop(0))
 
     swaps[0].start()
     swaps[1].start()
     for t in range(ahead):
         start(z_copies(t, t % 2 == 1))
-    swaps[2].start()
     own[0].wait()
     own[1].wait()
 
@@ -615,17 +629,17 @@
             result, _, _ = norm_rows(
                 x_out[half, rows, :].astype(jnp.float32), vectors[0:1, :], vectors[1:2, :]
             )
-            normed[half, rows, :] = result.astype(jnp.bfloat16)
+            normed[aligned(half * SLOTS + at * 64, 64, 64), :] = result.astype(jnp.bfloat16)
 
     norm_first(x)
     for m, ref in enumerate((mix_w, out_w, up_w, down_w)):
         squares[pl.ds(m, 1), :] = jnp.broadcast_to(square_sum(ref), (1, LANES))
-    link_step(0, False)
+    serve_some(1)
     swaps[0].wait_recv()
     swaps[1].wait_recv()
     norm_first(1 - x)
-    for t in range(1, 7):
-        link_step(t, t % 2 == 1)
+    serve_until(0)
+    swaps[2].start()
     valid = slots_valid(n_out, 1)
     lane = lax.broadcasted_iota(jnp.int32, (1, LANES), 1)
 
@@ -638,7 +652,9 @@
         v_bias = vectors[3:4, columns(pair * LANES, LANES)]
         bias = jnp.concatenate([q_bias, jnp.zeros_like(q_bias), v_bias], 1)
         for half in range(2):
-            qkv[pair, pl.ds(half * SLOTS, SLOTS), :] = (nn(normed[half], weights) + bias).astype(
+            qkv[pair, pl.ds(half * SLOTS, SLOTS), :] = (
+                nn(normed[pl.ds(half * SLOTS, SLOTS), :], weights) + bias
+            ).astype(
                 jnp.bfloat16
             )
 
@@ -662,10 +678,11 @@
             ).astype(jnp.bfloat16)
 
     for k in range(4):
+        serve_until(k)
         pair_task(0, k)
-        link_step(2 * k + 7, True)
+        serve_some(3)
         pair_task(1, k)
-        link_step(2 * k + 8, False)
+        serve_some(3)
 
     for tile in range(4):
         for half in range(2):
@@ -673,19 +690,83 @@
             cols = pl.ds(tile * 256, 256)
             branch = nt(heads[rows, :], wo[cols, :])
             hidden[rows, cols] = x_out[half, :, cols].astype(jnp.float32) + (branch + vectors[4:5, cols])
-        if tile < 3:
-            link_step(15 + tile, tile != 1)
+        serve_some(1)
 
     @pl.loop(0, ROWS // 64)
     def _(at):
         rows = pl.ds(pl.multiple_of(at * 64, 64), 64)
         result, _, _ = norm_rows(hidden[rows, :], vectors[5:6, :], vectors[6:7, :])
-        second[rows, :] = result.astype(jnp.bfloat16)
+        normed[rows, :] = result.astype(jnp.bfloat16)
+        total_acc[rows, :] = hidden[rows, :] + vectors[7:8, :]
 
     own[2].wait()
-    for k in range(CHUNKS):
+    swaps[2].wait_recv()
+    transpose_into(normed_t, normed)
+    for half in range(2):
+        for at in range(1024 // LANES):
+            lanes = pl.ds(at * LANES, LANES)
+            back_t[lanes, pl.ds(half * SLOTS, SLOTS)] = b_out[half, :, lanes].T
+    grad_second[...] = jnp.zeros_like(grad_second)
+
+    def send_tile(s):
+        j, side = (s // 2, s % 2) if isinstance(s, int) else (lax.div(s, 2), lax.rem(s, 2))
+        return pltpu.make_async_copy(staged, g_out.at[pl.ds(2 * j, 2), side], gs.at[0])
+
+    serve_until(5)
+    shares = {}
+    for s in range(7):
+        mark = len(events)
+        goal = [event for event in events if event[0] == 3 and event[1] <= 5 + 2 * ((s + 1) // 2)]
+        taken = max([events.index(event) + 1 for event in goal] + [0])
+        taken = max(taken, min(3, mark))
+        shares[s] = events[:taken]
+        del events[:taken]
+
+    @pl.loop(0, 8)
+    def _(s):
+        j, side = lax.div(s, 2), lax.rem(s, 2)
+        tile = side * 4 + j
+        bias = vectors[pl.ds(8 + side * 2 + lax.div(j, 2), 1), columns(lax.rem(j, 2) * WIDE, WIDE)]
+        up = w[4 + 2 * j, side].reshape(1024, WIDE)
+        down = w[5 + 2 * j, side].reshape(1024, WIDE)
+        sums = jnp.zeros((1, WIDE), jnp.float32)
+        for half in range(2):
+            rows = pl.ds(half * SLOTS, SLOTS)
+            pre = nn(normed[rows, :], up) + bias
+            grad_active = nn(b_out[half], down)
+            share = 0.5 * (1.0 + lax.erf(pre * 0.7071067811865476))
+            slope = share + pre * jnp.exp(-0.5 * pre * pre) * 0.3989422804014327
+            act = (pre * share).astype(low)
+            grad_pre = (grad_active * slope).astype(low)
+            halves[0, rows, :] = act
+            halves[1, rows, :] = grad_pre
+            sums += jnp.sum(grad_pre.astype(jnp.float32), 0, keepdims=True)
+            total_acc[rows, :] += nt(act, down)
+            grad_second[rows, :] += nt(grad_pre, up)
+        bias_grad[pl.ds(tile, 1), :] = sums
+
+        @pl.when(s > 0)
+        def _():
+            send_tile(s).wait()
+
+        for zi in range(2):
+            rows = pl.ds(zi * 512, 512)
+            staged[0, pl.ds(2 * zi, 2)] = nn(normed_t[rows, :], halves[1]).astype(low).reshape(2, 2, 128, WIDE)
+            staged[1, pl.ds(2 * zi, 2)] = nn(back_t[rows, :], halves[0]).astype(low).reshape(2, 2, 128, WIDE)
+        send_tile(s).start()
+        for done, calls in shares.items():
+            if calls:
+
+                @pl.when(s == done)
+                def _():
+                    for call in calls:
+                        serve(*call)
+
+    for half in range(2):
+        image_out[half] = total_acc[pl.ds(half * SLOTS, SLOTS), :].astype(low)
+    send_tile(7).wait()
+    for k in range(4):
         keep(k).wait()
-    swaps[2].wait_recv()
     for swap in swaps:
         swap.wait_send()
 
@@ -707,28 +788,36 @@
     return pl.pallas_call(
         front_body,
         out_shape=(
-            shape((CHUNKS, 2, 4, 2, 128, WIDE), low),
+            shape((4, 2, 4, 2, 128, WIDE), low),
+            shape((8, 2, 4, 2, 128, WIDE), low),
             shape((2, SLOTS, width), low),
             shape((2, SLOTS, width), low),
             shape((2, 8, LANES), full),
             shape((PAIRS, ROWS, 3 * LANES), low),
             shape((ROWS, width), low),
             shape((ROWS, width), full),
-            shape((ROWS, width), low),
             shape((8, LANES), full),
+            shape((ROWS, width), full),
+            shape((2, SLOTS, width), low),
+            shape((8, WIDE), full),
         ),
         in_specs=[anywhere] * 3 + [in_vmem] * 5,
-        out_specs=(anywhere, anywhere) + (in_vmem,) * 7,
+        out_specs=(anywhere, anywhere) + (in_vmem,) * 10,
         scratch_shapes=[
-            pltpu.VMEM((2, SLOTS, width), low),
+            pltpu.VMEM((ROWS, width), low),
             pltpu.VMEM((CHUNKS, 2, 4, 2, 128, WIDE), low),
             pltpu.VMEM((1024, 1024), low),
+            pltpu.VMEM((width, ROWS), low),
+            pltpu.VMEM((width, ROWS), low),
+            pltpu.VMEM((2, ROWS, WIDE), low),
+            pltpu.VMEM((ROWS, width), full),
+            pltpu.VMEM((2, 4, 2, 128, WIDE), low),
             dma((3,)), dma((3,)), dma((3,)), dma((CHUNKS, 3)), dma((CHUNKS, 3)),
             dma((CHUNKS, 2)), dma((CHUNKS, 2)), dma((CHUNKS, 4)), dma((CHUNKS, 4)), dma((CHUNKS, 4)), dma((CHUNKS, 4)),
-            dma((CHUNKS,)),
+            dma((4,)), dma((1,)),
         ],
         compiler_params=pltpu.CompilerParams(
-            collective_id=0, has_side_effects=True, vmem_limit_bytes=58 * MIB
+            collective_id=0, has_side_effects=True, vmem_limit_bytes=62 * MIB
         ),
     )(x_in, b_in, n_in, *weights, vectors)
 
@@ -751,17 +840,19 @@
         (
             self.g, self.cb, self.xa, self.ya, self.za, self.fa, self.yb, self.zb, self.xb, self.stage,
             self.cs, self.cr, self.s1s, self.s1r, self.s2s, self.s2r, self.s3s, self.s3r, self.s4s, self.s4r,
-            self.out_sem, self.free,
-        ) = refs[:22]
-        self.totals = refs[22:]
+            self.out_sem, self.free, self.in_sem, self.made,
+        ) = refs[:24]
+        self.totals = refs[24:]
         self.waited = set()
 
     def hops(self, stage, q):
         z, y, x, c = self.where
-        at, own = self.slot[q], self.g.at[q % 8]
+        at, own = self.slot[q], self.g.at[q]
         if stage == 0:
+            c = self.where[3]
+            source = self.made.at[q, 1 - c] if q < 8 else self.g.at[12 + q % 2]
             return [
-                remote(self.g.at[8 + q % 4], self.cb.at[q % 4], self.cs.at[q], self.cr.at[q], self.c_peer)
+                remote(source, self.cb.at[q % 4], self.cs.at[q], self.cr.at[q], self.c_peer)
             ]
         first, third = (self.s1s.at[q], self.s1r.at[q]), (self.s4s.at[q], self.s4r.at[q])
         second, last = (self.s2s.at[q], self.s2r.at[q]), (self.s3s.at[q], self.s3r.at[q])
@@ -806,17 +897,24 @@
                 copy.wait_send()
 
     def begin(self, q):
+        if q < 8:
+            self.load(q).start()
         if q >= 4:
             pl.semaphore_wait(self.free.at[q % 4], 1)
         self.start(0, q)
 
+    def load(self, q):
+        return pltpu.make_async_copy(self.made.at[q, self.where[3]], self.g.at[q], self.in_sem.at[q])
+
     def one(self, q):
+        if q < 8:
+            self.load(q).wait()
         self.arrive(0, q)
 
         @pl.loop(0, 8)
         def _(block):
             zi, yi = lax.div(block, 2), lax.rem(block, 2)
-            add_into(self.g, (q % 8, zi, yi), self.cb, (q % 4, zi, yi))
+            add_into(self.g, (q, zi, yi), self.cb, (q % 4, zi, yi))
 
         if q < 8:
             pl.semaphore_signal(
@@ -833,22 +931,22 @@
             @pl.loop(0, 8)
             def _(block):
                 zi, yi = lax.div(block, 2), lax.rem(block, 2)
-                add_into(self.g, (q % 8, zi, yi, self.near), self.xa, (at, zi, yi))
+                add_into(self.g, (q, zi, yi, self.near), self.xa, (at, zi, yi))
 
         else:
 
             @pl.loop(0, 4)
             def _(zi):
-                add_into(self.g, (q % 8, zi, y), self.yb, (at, zi))
+                add_into(self.g, (q, zi, y), self.yb, (at, zi))
 
         self.start(2, q)
 
     def sum_line(self, q, rows, buffer):
         z, y = self.where[:2]
-        value = self.g[(q % 8, z, y) + rows].astype(jnp.float32)
+        value = self.g[(q, z, y) + rows].astype(jnp.float32)
         for d in range(3):
             value += buffer[self.slot[q], d].astype(jnp.float32)
-        self.g[(q % 8, z, y) + rows] = value.astype(jnp.bfloat16)
+        self.g[(q, z, y) + rows] = value.astype(jnp.bfloat16)
 
     def three(self, q):
         y, at = self.where[1], self.slot[q]
@@ -857,7 +955,7 @@
 
             @pl.loop(0, 4)
             def _(zi):
-                add_into(self.g, (q % 8, zi, y, self.near), self.ya, (at, zi))
+                add_into(self.g, (q, zi, y, self.near), self.ya, (at, zi))
 
         else:
             self.sum_line(q, (), self.zb)
@@ -877,7 +975,7 @@
         else:
             if q >= 4:
                 self.export(q - 4).wait()
-            self.stage[q % 4] = self.g[q % 8, z, y].astype(jnp.float32) + self.xb[at].astype(jnp.float32)
+            self.stage[q % 4] = self.g[q, z, y].astype(jnp.float32) + self.xb[at].astype(jnp.float32)
             self.export(q).start()
 
     def five(self, q):
@@ -886,7 +984,7 @@
             self.arrive(4, q)
             if q >= 4:
                 self.export(q - 4).wait()
-            self.stage[q % 4, self.near] = self.g[q % 8, z, y, self.near].astype(jnp.float32)
+            self.stage[q % 4, self.near] = self.g[q, z, y, self.near].astype(jnp.float32)
             self.stage[q % 4, self.far] = self.fa[self.slot[q]].astype(jnp.float32)
             self.export(q).start()
 
@@ -909,7 +1007,7 @@
         n, across = len(crosswise), sum(crosswise)
         along = n - across
         return [
-            vmem((12, 4, 2, 128, WIDE), low),
+            vmem((14, 4, 2, 128, WIDE), low),
             vmem((4, 4, 2, 128, WIDE), low),
             vmem((across, 4, 2, 64, WIDE), low),
             vmem((across, 4, 64, WIDE), low),
@@ -920,7 +1018,7 @@
             vmem((along, 128, WIDE), low),
             vmem((4, 128, WIDE), jnp.float32),
             dma((n,)), dma((n,)), dma((n,)), dma((n,)), dma((n, 3)), dma((n, 3)),
-            dma((n, 3)), dma((n, 3)), dma((n,)), dma((n,)), dma((n,)), pltpu.SemaphoreType.REGULAR((4,)),
+            dma((n, 3)), dma((n, 3)), dma((n,)), dma((n,)), dma((n,)), pltpu.SemaphoreType.REGULAR((4,)), dma((8,)),
         ]
 
 
@@ -949,52 +1047,48 @@
         self.onward.wait()
 
 
-def transpose_into(target, source):
-    for at in range(source.shape[1] // LANES):
-        target[pl.ds(at * LANES, LANES), :] = source[:, pl.ds(at * LANES, LANES)].T
-
-
-KINDS = (True, False) * 4 + (True, False, False, False)
-
-
-def both(name, tile):
-    return ((name, 2 * tile), (name, 2 * tile + 1))
-
-
-MLP_PLAN = {
-    0: both("begin", 0),
-    1: both("one", 0),
-    2: both("begin", 1),
-    3: both("one", 1) + both("two", 0),
-    4: both("begin", 2),
-    5: both("one", 2),
-    6: both("begin", 3) + both("two", 1) + both("three", 0),
-    7: both("one", 3) + both("four", 0),
-}
-OUTPUT_PLAN = both("five", 0) + both("two", 2)
-NORM_PLAN = both("three", 1)
-PAIR_PLAN = {
-    0: (("begin", 8),) + both("four", 1) + both("two", 3),
-    1: (("one", 8),) + both("three", 2) + both("five", 1),
-    2: (("begin", 9),) + both("four", 2) + both("three", 3),
-    3: (("one", 9), ("two", 8)) + both("five", 2),
-    4: (("begin", 10),) + both("four", 3),
-    5: (("one", 10), ("two", 9), ("three", 8)) + both("five", 3),
-    6: (("begin", 11), ("three", 9), ("four", 8)),
-    7: (("one", 11), ("two", 10), ("four", 9)),
-}
-DRAIN_PLAN = (("five", 8), ("three", 10), ("two", 11), ("four", 10), ("three", 11), ("four", 11))
+KINDS = (False, False, False, True, True, True, True, True, False, True, False, False)
+PLAN = (
+    (("begin", 2), ("begin", 0), ("begin", 1), ("begin", 3),),
+    (),
+    (),
+    (("one", 2),),
+    (("begin", 6),),
+    (("one", 0),),
+    (("begin", 4),),
+    (("one", 1),),
+    (("begin", 5), ("one", 3),),
+    (("two", 2), ("begin", 7), ("one", 6),),
+    (("one", 4),),
+    (("two", 0), ("one", 5), ("two", 3), ("one", 7), ("begin", 8),),
+    (("three", 2),),
+    (("two", 1), ("two", 6), ("one", 8),),
+    (("begin", 9),),
+    (("three", 0), ("three", 3),),
+    (("one", 9), ("three", 6), ("two", 4),),
+    (("three", 1),),
+    (("begin", 10),),
+    (("four", 3), ("two", 5), ("two", 8),),
+    (("four", 6), ("one", 10), ("three", 4),),
+    (("three", 5), ("two", 7),),
+    (("four", 2), ("begin", 11), ("four", 0), ("three", 8),),
+    (("two", 10), ("four", 4),),
+    (("one", 11),),
+    (("four", 5), ("two", 9), ("four", 1), ("three", 7),),
+    (("five", 3), ("five", 6),),
+    (("five", 4), ("four", 8), ("two", 11), ("three", 10), ("three", 9), ("four", 7), ("five", 5), ("four", 10), ("three", 11), ("five", 7), ("four", 11), ("four", 9), ("five", 9),),
+)
 
 
 def back_body(
-    w, second_in, back_in, x_in, hidden_in, counts, qkv_in, heads_in, vectors,
-    total_m, total_q, out_spread, grad_spread, bias_grad, vec_out, qv_out,
-    tall, tall_t, back, back_t, halves, hidden, total_acc, grad_second, out_low, in_low, wv,
+    w, made, image_in, back_in, x_in, hidden_in, second_in, counts, qkv_in, heads_in, vectors,
+    total_m, total_q, out_spread, grad_spread, vec_out, qv_out,
+    tall, tall_t, back, back_t, hidden, total_acc, grad_second, out_low, in_low, wv,
     grad_part, parts, query_part, qkv_v, heads_v, vec_acc, *rest,
 ):
     ws, qs, hs, in_sems, out_sems, grad_sems = rest[:6]
     z, y, x, c = place()
-    rs = Scatter(KINDS, rest[6:] + (total_m, total_q))
+    rs = Scatter(KINDS, rest[6:] + (made, total_m, total_q))
     greet(rs.line + [rs.y_peer, rs.x_peer, rs.c_peer])
     low, full = jnp.bfloat16, jnp.float32
 
@@ -1003,16 +1097,12 @@
 
     def side_of(s):
         return lax.rem(1 - c + s, 2)
-
-    def tile_load(s):
-        slot, j = turn(s)
-        return pltpu.make_async_copy(w.at[pl.ds(4 + 2 * j, 2), side_of(s)], wv.at[slot], ws.at[slot])
 
     def pair_loads(s):
         slot, k = turn(s)
         pair = side_of(s) * 4 + k
         return [
-            pltpu.make_async_copy(w.at[k, side_of(s)], wv.at[slot, 0], ws.at[slot]),
+            pltpu.make_async_copy(w.at[k, side_of(s)], wv.at[slot], ws.at[slot]),
             pltpu.make_async_copy(qkv_in.at[pair], qkv_v.at[slot], qs.at[slot]),
             pltpu.make_async_copy(
                 heads_in.at[:, columns(pair * LANES, LANES)], heads_v.at[slot], hs.at[slot]
@@ -1026,85 +1116,26 @@
     loads = [
         pltpu.make_async_copy(src, dst, in_sems.at[at])
         for at, (src, dst) in enumerate(
-            ((second_in, tall), (back_in, back), (hidden_in, hidden), (x_in, in_low))
+            ((image_in, out_low), (second_in, grad_second), (hidden_in, hidden), (back_in, back), (x_in, in_low))
         )
     ]
-    start(loads[:3])
-    tile_load(0).start()
-    tile_load(1).start()
-    loads[3].start()
-    grad_second[...] = jnp.zeros_like(grad_second)
-    loads[0].wait()
-    transpose_into(tall_t, tall)
-    loads[1].wait()
-    transpose_into(back_t, back)
-    loads[2].wait()
-    total_acc[...] = hidden[...] + vectors[7:8, :]
-
-    @pl.loop(0, 8)
-    def _(s):
-        slot, j = turn(s)
-        side = side_of(s)
-        tile_load(s).wait()
-        tile = side * 4 + j
-        bias = vectors[pl.ds(8 + side * 2 + lax.div(j, 2), 1), columns(lax.rem(j, 2) * WIDE, WIDE)]
-        up = wv[slot, 0].reshape(1024, WIDE)
-        down = wv[slot, 1].reshape(1024, WIDE)
-        sums = jnp.zeros((1, WIDE), full)
-        for half in range(2):
-            rows = pl.ds(half * SLOTS, SLOTS)
-            pre = nn(tall[rows, :], up) + bias
-            grad_active = nn(back[rows, :], down)
-            share = 0.5 * (1.0 + lax.erf(pre * 0.7071067811865476))
-            slope = share + pre * jnp.exp(-0.5 * pre * pre) * 0.3989422804014327
-            act = (pre * share).astype(low)
-            grad_pre = (grad_active * slope).astype(low)
-            halves[0, rows, :] = act
-            halves[1, rows, :] = grad_pre
-            sums += jnp.sum(grad_pre.astype(full), 0, keepdims=True)
-            total_acc[rows, :] += nt(act, down)
-            grad_second[rows, :] += nt(grad_pre, up)
-        bias_grad[pl.ds(tile, 1), :] = sums
-        for again in (4, 6):
-
-            @pl.when(s == again)
-            def _():
-                rs.sent(again - 4, (0,))
-                rs.sent(again - 3, (0,))
-
-        first = jnp.where(slot == 0, 8 + lax.rem(2 * j, 4), 2 * j)
-        for zi in range(4):
-            rows = pl.ds(zi * 256, 256)
-            rs.g[first, zi] = nn(tall_t[rows, :], halves[1]).astype(low).reshape(2, 128, WIDE)
-            rs.g[first + 1, zi] = nn(back_t[rows, :], halves[0]).astype(low).reshape(2, 128, WIDE)
-
-        @pl.when(s < 6)
-        def _():
-            tile_load(s + 2).start()
-
-        for done, calls in MLP_PLAN.items():
-
-            @pl.when(s == done)
-            def _():
-                rs.run(calls)
-
+    rs.run(PLAN[0])
+    start(loads)
     start(pair_loads(0))
     start(pair_loads(1))
     sent_out = Spread(out_low, out_spread, out_sems)
-    for first in (True, False):
-        half = 1 - x if first else x
-        out_low[half] = total_acc[aligned(half * SLOTS, SLOTS, SLOTS), :].astype(low)
-        if first:
-            sent_out.cross.start()
+    loads[0].wait()
+    sent_out.cross.start()
     sent_out.start()
-    rs.run(OUTPUT_PLAN)
+    rs.run(PLAN[1])
     vec_acc[...] = jnp.zeros_like(vec_acc)
 
     def fold(row, value):
         vec_acc[row] += jnp.sum(value.reshape(-1, 8, value.shape[1]), 0)
 
     step = 64
-    loads[3].wait()
+    for load in loads[1:]:
+        load.wait()
 
     @pl.loop(0, ROWS // step)
     def _(at):
@@ -1126,11 +1157,18 @@
             in_low[lax.div(at, 5), half_rows, :].astype(full), vectors[0:1, :], vectors[1:2, :]
         )
         tall[rows, :] = first.astype(low)
+        for turn_at in range(5):
+            if PLAN[2 + turn_at]:
+
+                @pl.when(at == 2 * turn_at + 1)
+                def _():
+                    rs.run(PLAN[2 + turn_at])
 
     transpose_into(back_t, back)
+    rs.run(PLAN[7])
     transpose_into(tall_t, tall)
     total_acc[...] = jnp.zeros_like(total_acc)
-    rs.run(NORM_PLAN)
+    rs.run(PLAN[8])
     sent_out.forward()
     valid = slots_valid(counts, 0)
     lane = lax.broadcasted_iota(jnp.int32, (1, LANES), 1)
@@ -1142,7 +1180,7 @@
         pair = side_of(s) * 4 + k
         for copy in pair_loads(s):
             copy.wait()
-        grad_heads = nn(back[...], wv[slot, 0, :, :, :, pl.ds(3 * LANES, LANES)].reshape(1024, LANES))
+        grad_heads = nn(back[...], wv[slot, :, :, :, pl.ds(3 * LANES, LANES)].reshape(1024, LANES))
         grad_heads = grad_heads.astype(low)
         queries = qkv_v[slot, :, pl.ds(0, LANES)]
         keys = qkv_v[slot, :, pl.ds(LANES, LANES)]
@@ -1168,6 +1206,13 @@
             parts[0] += jnp.where(here, nn(grad_scores, queries), 0.0)
             parts[1] += jnp.where(here, nn(attention.astype(low), grad_heads), 0.0)
 
+        for done in range(8):
+            if PLAN[9 + 2 * done]:
+
+                @pl.when(s == done)
+                def _():
+                    rs.run(PLAN[9 + 2 * done])
+
         grad_q = (query_part[...] * 0.125).T.astype(low)
         grad_k = (parts[0] * 0.125).astype(low)
         grad_v = parts[1].astype(low)
@@ -1179,37 +1224,35 @@
         for half in range(2):
             rows = pl.ds(half * SLOTS, SLOTS)
             total_acc[rows, :] += nt(
-                grad_part[rows, :], wv[slot, 0, :, :, :, pl.ds(0, 3 * LANES)].reshape(1024, 3 * LANES)
+                grad_part[rows, :], wv[slot, :, :, :, pl.ds(0, 3 * LANES)].reshape(1024, 3 * LANES)
             )
-        for again in range(4):
+        for again in (2, 3):
 
             @pl.when(s == 2 * again)
             def _():
-                rs.sent(4 + again, (0,))
-
-            @pl.when(s == 2 * again + 1)
-            def _():
-                rs.sent(again, (1, 2, 3, 4))
-
-        target = jnp.where(slot == 0, 8 + k, k)
-        for zi in range(4):
-            rows = pl.ds(zi * 256, 256)
-            rs.g[target, zi, :, :, pl.ds(0, 3 * LANES)] = (
-                nn(tall_t[rows, :], grad_part[...]).astype(low).reshape(2, 128, 3 * LANES)
+                rs.sent(6 + again, (0,))
+
+        target = jnp.where(slot == 0, 12 + lax.rem(k, 2), 8 + k)
+        for zi in range(2):
+            rows = pl.ds(zi * 512, 512)
+            blocks = pl.ds(2 * zi, 2)
+            rs.g[target, blocks, :, :, pl.ds(0, 3 * LANES)] = (
+                nn(tall_t[rows, :], grad_part[...]).astype(low).reshape(2, 2, 128, 3 * LANES)
             )
-            rs.g[target, zi, :, :, pl.ds(3 * LANES, LANES)] = (
-                nn(back_t[rows, :], heads_v[slot]).astype(low).reshape(2, 128, LANES)
+            rs.g[target, blocks, :, :, pl.ds(3 * LANES, LANES)] = (
+                nn(back_t[rows, :], heads_v[slot]).astype(low).reshape(2, 2, 128, LANES)
             )
 
         @pl.when(s < 6)
         def _():
             start(pair_loads(s + 2))
 
-        for done, calls in PAIR_PLAN.items():
-
-            @pl.when(s == done)
-            def _():
-                rs.run(calls)
+        for done in range(8):
+            if PLAN[10 + 2 * done]:
+
+                @pl.when(s == done)
+                def _():
+                    rs.run(PLAN[10 + 2 * done])
 
     sent_grad = Spread(in_low, grad_spread, grad_sems)
     for first in (True, False):
@@ -1229,23 +1272,24 @@
 
         if first:
             sent_grad.cross.start()
+            rs.run(PLAN[25])
     sent_grad.start()
     for row in range(6):
         vec_out[pl.ds(row, 1), :] = jnp.sum(vec_acc[row], 0, keepdims=True)
-    rs.run(DRAIN_PLAN)
+    rs.run(PLAN[26] + PLAN[27])
     sent_grad.forward()
     sent_out.finish()
     sent_grad.finish()
     rs.finish()
 
 
-def back_all(w, second, back, x_all, hidden, counts, qkv, heads, vectors):
+def back_all(w, made, image, back, x_all, hidden, grad_second, counts, qkv, heads, vectors):
     dma, vmem = pltpu.SemaphoreType.DMA, pltpu.VMEM
     low, full = jnp.bfloat16, jnp.float32
     anywhere = pl.BlockSpec(memory_space=pl.ANY)
     in_vmem = pl.BlockSpec(memory_space=pltpu.VMEM)
     shape = jax.ShapeDtypeStruct
-    width = second.shape[1]
+    width = hidden.shape[1]
     return pl.pallas_call(
         back_body,
         out_shape=(
@@ -1253,36 +1297,34 @@
             shape((4, 128, WIDE), full),
             shape((4, SLOTS, width), low),
             shape((4, SLOTS, width), low),
-            shape((8, WIDE), full),
             shape((8, width), full),
             shape((16, LANES), full),
         ),
-        in_specs=[anywhere] * 5 + [in_vmem] + [anywhere] * 2 + [in_vmem],
-        out_specs=(anywhere,) * 4 + (in_vmem,) * 3,
+        in_specs=[anywhere] * 7 + [in_vmem] + [anywhere] * 2 + [in_vmem],
+        out_specs=(anywhere,) * 4 + (in_vmem,) * 2,
         scratch_shapes=[
             vmem((ROWS, width), low),
             vmem((width, ROWS), low),
             vmem((ROWS, width), low),
             vmem((width, ROWS), low),
-            vmem((2, ROWS, WIDE), low),
             vmem((ROWS, width), full),
             vmem((ROWS, width), full),
             vmem((ROWS, width), full),
             vmem((2, SLOTS, width), low),
             vmem((2, SLOTS, width), low),
-            vmem((2, 2, 4, 2, 128, WIDE), low),
+            vmem((2, 4, 2, 128, WIDE), low),
             vmem((ROWS, 3 * LANES), low),
             vmem((2, ROWS, LANES), full),
             vmem((LANES, ROWS), full),
             vmem((2, ROWS, 3 * LANES), low),
             vmem((2, ROWS, LANES), low),
             vmem((6, 8, width), full),
-            dma((2,)), dma((2,)), dma((2,)), dma((4,)), dma((7,)), dma((7,)),
+            dma((2,)), dma((2,)), dma((2,)), dma((5,)), dma((7,)), dma((7,)),
         ] + Scatter.scratch(KINDS),
         compiler_params=pltpu.CompilerParams(
             collective_id=1, has_side_effects=True, vmem_limit_bytes=62 * MIB
         ),
-    )(w, second, back, x_all, hidden, counts, qkv, heads, vectors)
+    )(w, made, image, back, x_all, hidden, grad_second, counts, qkv, heads, vectors)
 
 
 TILES = (
@@ -1567,11 +1609,11 @@
     counts = jnp.sum(key_mask, 1).astype(jnp.float32)
     n_in = jnp.broadcast_to(counts[:, None, None], (images, 8, LANES))
     weights = (qkv_weight.transpose(1, 0, 2), out_weight, up_weight, down_weight)
-    w, b_all, x_all, n_all, qkv, heads, hidden, second, squares = front_all(
+    w, made, b_all, x_all, n_all, qkv, heads, hidden, squares, grad_second, image, bias_grad = front_all(
         x_in, b_in, n_in, weights, vectors
     )
-    total_m, total_q, out_spread, grad_spread, bias_grad, vec_sums, qv_sums = back_all(
-        w, second, b_all.reshape(ROWS, width), x_all, hidden, n_all, qkv, heads, vectors
+    total_m, total_q, out_spread, grad_spread, vec_sums, qv_sums = back_all(
+        w, made, image, b_all.reshape(ROWS, width), x_all, hidden, grad_second, n_all, qkv, heads, vectors
     )
     factors = factor_all(
         total_q, total_m, squares, vec_sums, qv_sums, bias_grad, vectors, vector_moments,

time: 388 us -> 373 us (0.961)
  Pallas kernels: 365 us -> 350 us
    pallas_call x1, Pallas kernels: 191 us -> 142 us  [back_all(): pl.pallas_call(back_body, out_shape=(shape((8, 128, WIDE), full), shape((...]
    pallas_call x1, Pallas kernels: 140 us -> 177 us  [front_all(): pl.pallas_call(front_body, out_shape=(shape((4, 2, 4, 2, 128, WIDE), low)...]
    pallas_call x1, Pallas kernels: 30.8 us -> 26.7 us  [factor_all(): pl.pallas_call(factor_body, out_shape=tuple((shape(one, full) for one in...]
where the time goes in v2:
time: 373 us; the launch traced here: 370 us
  Pallas kernels  350 us (94%)
  local copies, waits for them, and re-layouts  14.6 us (4%)
  other arithmetic  3.94 us (1%)
    pallas_call x1, Pallas kernels, front_all(): pl.pallas_call(front_body, out_shape=(shape((4, 2, 4, 2, 128, WIDE), low)...  177 us
    pallas_call x1, Pallas kernels, back_all(): pl.pallas_call(back_body, out_shape=(shape((8, 128, WIDE), full), shape((...  142 us
    pallas_call x1, Pallas kernels, factor_all(): pl.pallas_call(factor_body, out_shape=tuple((shape(one, full) for one in...  26.7 us
    unnamed x47, local copies, waits for them, and re-layouts  8.21 us

profile of v2, /device:TPU:0, one launch (start us, length us, event | category | flops | bytes accessed | tf_op | source)
XLA Modules:
  0.0 369.8 jit_solution(9084512266491440447)
XLA Ops:
  0.7 0.9 fusion
  1.6 0.7 broadcast_in_dim.2.n_in
  2.2 3.1 copy_multiply_fusion
  5.3 0.0 copy-start.20
  5.3 1.7 pad.8.b_in
  7.0 0.9 copy-done.20
  7.9 0.7 copy.43
  8.7 1.8 pad.7.x_in
  10.4 176.9 %shard_map.369 = (bf16[4,2,4,2,128,512]{5,4,3,2,1,0:T(8,128)(2,1)}, bf16[8,2,4,2,128,512]{5,4,3,2,1,0:T(8,128)(2,1)}, bf16[2,320,1024]{2,1,0:T(8,128)(2,1)}, bf1...) custom-call(bf16[4,320,1024]{2,1,0:T(8,128)(2,1)} %pad.7.x_in, ...), custom_call_target="tpu_custom_call" | custom-call | tf_op jit(solution)/shard_map/pallas_call | solution.py:788
  187.3 142.3 %shard_map.370 = (f32[8,128,512]{2,1,0:T(8,128)}, f32[4,128,512]{2,1,0:T(8,128)}, bf16[4,320,1024]{2,1,0:T(8,128)(2,1)}, bf16[4,320,1024]{2,1,0:T(8,128)(2,1)}, f32[8,1024]{1,0:T(8,128)}, /*index=5*/f32[16,128]{1,0:T(8,128)}) custom-call(bf16[4,2,4,2,128,512]{5,4,3,2,1,0:T(8,128)(2,1)} %get-tuple-element.76.w, ...), custom_call_target="tpu_custom_call" | custom-call | tf_op jit(solution)/shard_map/pallas_call | solution.py:1293
  329.7 1.9 slice.6
  331.6 0.0 copy-start.6
  331.6 0.0 copy-start.7
  331.7 0.0 copy-start.10
  331.7 0.0 copy-start.11
  331.7 0.0 copy-start.16
  331.7 0.0 copy-start.17
  331.8 3.2 copy.45
  335.2 26.7 %shard_map.371 = (f32[128,128]{1,0:T(8,128)S(1)}, f32[128,128]{1,0:T(8,128)S(1)}, f32[3,512]{1,0:T(4,128)S(1)}, f32[4,128]{1,0:T(4,128)S(1)}, f32[16,128]{1,0:T(...) custom-call(f32[4,128,512]{2,1,0:T(8,128)S(1)} %copy-done.1, ...), custom_call_target="tpu_custom_call" | custom-call | tf_op jit(solution)/shard_map/pallas_call | solution.py:1502
  361.9 0.2 slice.7
  362.2 0.0 copy-start.2
  362.2 0.0 copy-start.5
  362.2 3.2 copy.46
  365.5 4.0 %shard_map.372 = (f32[3,128,512]{2,1,0:T(8,128)}, f32[512,128]{1,0:T(8,128)}, f32[128,2048]{1,0:T(8,128)}, f32[2048,128]{1,0:T(8,128)}, f32[3,128,512]{2,1,0:T(8...) custom-call(f32[4,128,512]{2,1,0:T(8,128)S(1)} %copy-done.1, ...), custom_call_target="tpu_custom_call" | custom-call | tf_op jit(solution)/shard_map/pallas_call | solution.py:1587
  (35 shorter events, 0.1 us)
Async XLA Ops:
  5.3 2.6 copy-start.20
  331.6 3.4 copy-start
  331.6 3.4 copy-start.1
  331.6 3.4 copy-start.6
  331.6 3.4 copy-start.7
  331.6 3.4 copy-start.8
  331.7 3.4 copy-start.9
  331.7 3.4 copy-start.10
  331.7 3.4 copy-start.11
  331.7 3.4 copy-start.12
  331.7 3.4 copy-start.13
  331.7 3.4 copy-start.14
  331.7 3.4 copy-start.15
  331.7 3.4 copy-start.16
  331.7 3.4 copy-start.17
  331.8 3.4 copy-start.18
  331.8 3.4 copy-start.19
  335.2 26.8 %copy-start.21 = (bf16[4,320,1024]{2,1,0:T(8,128)(2,1)S(1)}, bf16[4,320,1024]{2,1,0:T(8,128)(2,1)}, u32[]{:S(2)}) copy-start(bf16[4,320,1024]{2,1,0:T(8,128)(2,1)} %get-tuple-element.87) | copy-start | bytes 7864324
  362.2 3.3 copy-start.2
  362.2 3.3 copy-start.3
  362.2 3.3 copy-start.4
  362.2 3.3 copy-start.5

commit v3 on v2

--- a/solution.py
+++ b/solution.py
@@ -508,12 +508,52 @@
     return jnp.sum(total, 1, keepdims=True)
 
 
-def arrival_time(event):
-    kind, k = event
-    return k + kind * (1.1 if k < 2 else 2.1)
-
-
-ARRIVALS = sorted(((kind, k) for k in range(CHUNKS) for kind in range(4)), key=arrival_time)
+SERVE = (
+    (),
+    ((0, 0), (0, 1), (0, 2), (1, 0), (0, 3), (1, 1), (2, 0), (1, 2), (0, 4), (3, 0),),
+    (),
+    ((2, 1),),
+    (),
+    ((1, 3), (0, 5),),
+    ((3, 1),),
+    (),
+    ((2, 2), (1, 4),),
+    (),
+    ((0, 6),),
+    ((3, 2),),
+    (),
+    ((1, 5), (2, 3),),
+    (),
+    ((0, 7),),
+    ((1, 6), (3, 3), (2, 4),),
+    (),
+    (),
+    (),
+    ((3, 4),),
+    ((0, 8), (1, 7),),
+    (),
+    (),
+    (),
+    (),
+    ((0, 9), (1, 8),),
+    ((2, 5), (0, 10), (2, 6), (3, 5),),
+    ((1, 9),),
+    ((2, 7), (3, 6),),
+    ((0, 11),),
+    ((1, 10), (2, 8), (3, 7),),
+    (),
+    ((2, 9),),
+    ((3, 8), (1, 11),),
+    ((2, 10), (3, 9),),
+    (),
+    ((2, 11),),
+    ((3, 10),),
+    ((3, 11),),
+    (),
+    (),
+    (),
+    (),
+)
 
 
 def transpose_into(target, source):
@@ -552,21 +592,21 @@
         for at, (src, dst) in enumerate(pairs)
     ]
 
-    def share(odd):
-        size = 96
+    def share(k):
+        size = 80 if k < 6 else 96
         return aligned(x * (128 - size), size, 16), aligned(x * size, 128 - size, 16)
 
-    def z_copies(k, odd):
-        block = w.at[k, c, z, y, share(odd)[0]]
+    def z_copies(k):
+        block = w.at[k, c, z, y, share(k)[0]]
         return [remote(block, block, zs.at[k, at], zr.at[k, at], peer) for at, peer in enumerate(line)]
 
-    def y_copies(k, odd):
-        rows = share(odd)[0]
+    def y_copies(k):
+        rows = share(k)[0]
         blocks = [w.at[k, c, pl.ds(2 * at, 2), y, rows] for at in range(2)]
         return [remote(block, block, ys.at[k, at], yr.at[k, at], y_peer) for at, block in enumerate(blocks)]
 
-    def x_copies(k, odd):
-        rows = share(odd)[1]
+    def x_copies(k):
+        rows = share(k)[1]
         blocks = [w.at[k, c, at, :, rows] for at in range(4)]
         return [remote(block, block, xs.at[k, at], xr.at[k, at], x_peer) for at, block in enumerate(blocks)]
 
@@ -585,40 +625,35 @@
         for copy in copies:
             copy.wait_recv()
 
-    ahead = 2
+    ahead = 3
 
     def serve(kind, k):
-        odd = k % 2 == 1
         if kind == 0:
-            arrive(z_copies(k, odd))
-            start(y_copies(k, odd))
+            arrive(z_copies(k))
+            start(y_copies(k))
             if k + ahead < CHUNKS:
-                start(z_copies(k + ahead, odd))
+                start(z_copies(k + ahead))
         elif kind == 1:
-            arrive(y_copies(k, odd))
-            start(x_copies(k, odd))
+            arrive(y_copies(k))
+            start(x_copies(k))
         elif kind == 2:
-            arrive(x_copies(k, odd))
+            arrive(x_copies(k))
             start(c_copies(k))
         else:
             arrive(c_copies(k))
             if k < 4:
                 keep(k).start()
 
-    events = list(ARRIVALS)
-
-    def serve_some(count):
-        for _ in range(min(count, len(events))):
-            serve(*events.pop(0))
-
-    def serve_until(k):
-        while (3, k) in events:
-            serve(*events.pop(0))
+    def hook(at):
+        for call in SERVE[at]:
+            serve(*call)
+        if at == 8:
+            swaps[2].start()
 
     swaps[0].start()
     swaps[1].start()
     for t in range(ahead):
-        start(z_copies(t, t % 2 == 1))
+        start(z_copies(t))
     own[0].wait()
     own[1].wait()
 
@@ -634,12 +669,11 @@
     norm_first(x)
     for m, ref in enumerate((mix_w, out_w, up_w, down_w)):
         squares[pl.ds(m, 1), :] = jnp.broadcast_to(square_sum(ref), (1, LANES))
-    serve_some(1)
+    hook(0)
     swaps[0].wait_recv()
     swaps[1].wait_recv()
     norm_first(1 - x)
-    serve_until(0)
-    swaps[2].start()
+    hook(1)
     valid = slots_valid(n_out, 1)
     lane = lax.broadcasted_iota(jnp.int32, (1, LANES), 1)
 
@@ -657,6 +691,8 @@
             ).astype(
                 jnp.bfloat16
             )
+
+        hook(3 + 5 * k + 2 * side)
 
         @pl.loop(0, 2)
         def _(half):
@@ -678,11 +714,11 @@
             ).astype(jnp.bfloat16)
 
     for k in range(4):
-        serve_until(k)
+        hook(2 + 5 * k)
         pair_task(0, k)
-        serve_some(3)
+        hook(4 + 5 * k)
         pair_task(1, k)
-        serve_some(3)
+        hook(6 + 5 * k)
 
     for tile in range(4):
         for half in range(2):
@@ -690,7 +726,7 @@
             cols = pl.ds(tile * 256, 256)
             branch = nt(heads[rows, :], wo[cols, :])
             hidden[rows, cols] = x_out[half, :, cols].astype(jnp.float32) + (branch + vectors[4:5, cols])
-        serve_some(1)
+        hook(22 + tile)
 
     @pl.loop(0, ROWS // 64)
     def _(at):
@@ -701,6 +737,7 @@
 
     own[2].wait()
     swaps[2].wait_recv()
+    hook(26)
     transpose_into(normed_t, normed)
     for half in range(2):
         for at in range(1024 // LANES):
@@ -712,15 +749,15 @@
         j, side = (s // 2, s % 2) if isinstance(s, int) else (lax.div(s, 2), lax.rem(s, 2))
         return pltpu.make_async_copy(staged, g_out.at[pl.ds(2 * j, 2), side], gs.at[0])
 
-    serve_until(5)
-    shares = {}
-    for s in range(7):
-        mark = len(events)
-        goal = [event for event in events if event[0] == 3 and event[1] <= 5 + 2 * ((s + 1) // 2)]
-        taken = max([events.index(event) + 1 for event in goal] + [0])
-        taken = max(taken, min(3, mark))
-        shares[s] = events[:taken]
-        del events[:taken]
+    hook(27)
+
+    def hooks_at(s, first):
+        for done in range(8):
+            if SERVE[first + 2 * done]:
+
+                @pl.when(s == done)
+                def _():
+                    hook(first + 2 * done)
 
     @pl.loop(0, 8)
     def _(s):
@@ -744,6 +781,7 @@
             total_acc[rows, :] += nt(act, down)
             grad_second[rows, :] += nt(grad_pre, up)
         bias_grad[pl.ds(tile, 1), :] = sums
+        hooks_at(s, 28)
 
         @pl.when(s > 0)
         def _():
@@ -754,13 +792,7 @@
             staged[0, pl.ds(2 * zi, 2)] = nn(normed_t[rows, :], halves[1]).astype(low).reshape(2, 2, 128, WIDE)
             staged[1, pl.ds(2 * zi, 2)] = nn(back_t[rows, :], halves[0]).astype(low).reshape(2, 2, 128, WIDE)
         send_tile(s).start()
-        for done, calls in shares.items():
-            if calls:
-
-                @pl.when(s == done)
-                def _():
-                    for call in calls:
-                        serve(*call)
+        hooks_at(s, 29)
 
     for half in range(2):
         image_out[half] = total_acc[pl.ds(half * SLOTS, SLOTS), :].astype(low)
@@ -770,12 +802,9 @@
     for swap in swaps:
         swap.wait_send()
 
-    @pl.loop(0, CHUNKS // 2)
-    def _(at):
-        for odd in (False, True):
-            k = 2 * at + int(odd)
-            for copy in z_copies(k, odd) + y_copies(k, odd) + x_copies(k, odd) + c_copies(k):
-                copy.wait_send()
+    for k in range(CHUNKS):
+        for copy in z_copies(k) + y_copies(k) + x_copies(k) + c_copies(k):
+            copy.wait_send()
 
 
 def front_all(x_in, b_in, n_in, weights, vectors):

time: 373 us -> 355 us (0.952)
  Pallas kernels: 350 us -> 332 us
    pallas_call x1, Pallas kernels: 177 us -> 158 us  [front_all(): pl.pallas_call(front_body, out_shape=(shape((4, 2, 4, 2, 128, WIDE), low)...]
    pallas_call x1, Pallas kernels: 26.7 us -> 30.7 us  [factor_all(): pl.pallas_call(factor_body, out_shape=tuple((shape(one, full) for one in...]
where the time goes in v3:
time: 355 us; the launch traced here: 352 us
  Pallas kernels  332 us (94%)
  local copies, waits for them, and re-layouts  14.6 us (4%)
  other arithmetic  3.94 us (1%)
    pallas_call x1, Pallas kernels, front_all(): pl.pallas_call(front_body, out_shape=(shape((4, 2, 4, 2, 128, WIDE), low)...  158 us
    pallas_call x1, Pallas kernels, back_all(): pl.pallas_call(back_body, out_shape=(shape((8, 128, WIDE), full), shape((...  140 us
    pallas_call x1, Pallas kernels, factor_all(): pl.pallas_call(factor_body, out_shape=tuple((shape(one, full) for one in...  30.7 us
    unnamed x47, local copies, waits for them, and re-layouts  8.21 us

profile of v3, /device:TPU:0, one launch (start us, length us, event | category | flops | bytes accessed | tf_op | source)
XLA Modules:
  0.0 352.3 jit_solution(2356389963621105502)
XLA Ops:
  0.7 0.9 fusion
  1.6 0.7 broadcast_in_dim.2.n_in
  2.2 3.1 copy_multiply_fusion
  5.3 1.7 pad.8.b_in
  7.0 0.9 copy-done.20
  7.9 0.7 copy.43
  8.7 1.8 pad.7.x_in
  10.4 158.2 %shard_map.369 = (bf16[4,2,4,2,128,512]{5,4,3,2,1,0:T(8,128)(2,1)}, bf16[8,2,4,2,128,512]{5,4,3,2,1,0:T(8,128)(2,1)}, bf16[2,320,1024]{2,1,0:T(8,128)(2,1)}, bf1...) custom-call(bf16[4,320,1024]{2,1,0:T(8,128)(2,1)} %pad.7.x_in, ...), custom_call_target="tpu_custom_call" | custom-call | tf_op jit(solution)/shard_map/pallas_call | solution.py:817
  168.7 139.5 %shard_map.370 = (f32[8,128,512]{2,1,0:T(8,128)}, f32[4,128,512]{2,1,0:T(8,128)}, bf16[4,320,1024]{2,1,0:T(8,128)(2,1)}, bf16[4,320,1024]{2,1,0:T(8,128)(2,1)}, f32[8,1024]{1,0:T(8,128)}, /*index=5*/f32[16,128]{1,0:T(8,128)}) custom-call(bf16[4,2,4,2,128,512]{5,4,3,2,1,0:T(8,128)(2,1)} %get-tuple-element.76.w, ...), custom_call_target="tpu_custom_call" | custom-call | tf_op jit(solution)/shard_map/pallas_call | solution.py:1322
  308.2 1.9 slice.6
  310.2 0.0 copy-start.6
  310.2 0.0 copy-start.7
  310.2 0.0 copy-start.11
  310.2 0.0 copy-start.12
  310.3 0.0 copy-start.17
  310.3 0.0 copy-start.18
  310.3 3.2 copy.45
  313.7 30.7 %shard_map.371 = (f32[128,128]{1,0:T(8,128)S(1)}, f32[128,128]{1,0:T(8,128)S(1)}, f32[3,512]{1,0:T(4,128)S(1)}, f32[4,128]{1,0:T(4,128)S(1)}, f32[16,128]{1,0:T(...) custom-call(f32[4,128,512]{2,1,0:T(8,128)S(1)} %copy-done.1, ...), custom_call_target="tpu_custom_call" | custom-call | tf_op jit(solution)/shard_map/pallas_call | solution.py:1531
  344.4 0.2 slice.7
  344.6 0.0 copy-start.2
  344.6 0.0 copy-start.3
  344.7 0.0 copy-start.5
  344.7 3.2 copy.46
  347.9 4.0 %shard_map.372 = (f32[3,128,512]{2,1,0:T(8,128)}, f32[512,128]{1,0:T(8,128)}, f32[128,2048]{1,0:T(8,128)}, f32[2048,128]{1,0:T(8,128)}, f32[3,128,512]{2,1,0:T(8...) custom-call(f32[4,128,512]{2,1,0:T(8,128)S(1)} %copy-done.1, ...), custom_call_target="tpu_custom_call" | custom-call | tf_op jit(solution)/shard_map/pallas_call | solution.py:1616
  (35 shorter events, 0.1 us)
Async XLA Ops:
  5.3 2.6 copy-start.20
  310.1 3.4 copy-start
  310.1 3.4 copy-start.1
  310.2 3.4 copy-start.6
  310.2 3.4 copy-start.7
  310.2 3.4 copy-start.8
  310.2 3.4 copy-start.9
  310.2 3.4 copy-start.10
  310.2 3.4 copy-start.11
  310.2 3.4 copy-start.12
  310.2 3.4 copy-start.13
  310.2 3.4 copy-start.14
  310.3 3.4 copy-start.15
  310.3 3.4 copy-start.16
  310.3 3.4 copy-start.17
  310.3 3.4 copy-start.18
  310.3 3.4 copy-start.19
  313.7 30.7 %copy-start.21 = (bf16[4,320,1024]{2,1,0:T(8,128)(2,1)S(1)}, bf16[4,320,1024]{2,1,0:T(8,128)(2,1)}, u32[]{:S(2)}) copy-start(bf16[4,320,1024]{2,1,0:T(8,128)(2,1)} %get-tuple-element.87) | copy-start | bytes 7864324
  344.6 3.3 copy-start.2
  344.6 3.3 copy-start.3
  344.7 3.3 copy-start.4
  344.7 3.3 copy-start.5
